TPU v7x, 32 devices: a whole 2x2x4 slice. The times are simulated.
32 devices in a mesh: dp: 8 (over y, x, core), tensor: 4 (over z).
Axes of the slice: x: 2, y: 2, z: 4, core: 2. Of those that a mesh axis runs over, the one named last changes fastest.
Arguments:
- residual: bfloat16 [8192, 2048], P(('dp', 'tensor')), may hold values from -6 to 6
- segments: int32 [8, 1024], P('dp'), may hold values from 0 to 7, never falling along the last dimension, each value on 1 to 512 neighbouring positions
- mixgain: bfloat16 [2048], P(('dp', 'tensor')), may hold values from 0.5 to 1.5
- ffngain: bfloat16 [2048], P(('dp', 'tensor')), may hold values from 0.5 to 1.5
- gateproj: bfloat16 [2048, 3072], P('dp', 'tensor'), may hold values from -0.125 to 0.125
- innerproj: bfloat16 [2048, 3072], P('dp', 'tensor'), may hold values from -0.125 to 0.125
- stepproj: bfloat16 [2048, 48], P('dp', 'tensor'), may hold values from -0.125 to 0.125
- sharedproj: bfloat16 [2048, 512], P(('dp', 'tensor')), may hold values from -0.125 to 0.125
- innerconv: bfloat16 [3072, 4], P('tensor'), may hold values from -1.796875 to 1.796875
- sharedconv: bfloat16 [512, 4], P(('dp', 'tensor')), may hold values from -1.796875 to 1.796875
- stepbias: bfloat16 [48], P('tensor'), may hold values from -6 to -2
- decaylog: bfloat16 [48], P('tensor'), may hold values from -4 to 0
- skipgain: bfloat16 [48], P('tensor'), may hold values from 0.5 to 1.5
- mixerout: bfloat16 [2048, 3072], P('dp', 'tensor'), may hold values from -0.109375 to 0.109375
- queryproj: bfloat16 [2048, 1024], P('dp', 'tensor'), may hold values from -0.125 to 0.125
- keyvalue: bfloat16 [2048, 512], P(('dp', 'tensor')), may hold values from -0.125 to 0.125
- attnout: bfloat16 [2048, 1024], P('dp', 'tensor'), may hold values from -0.375 to 0.375
- ffngate: bfloat16 [2048, 4096], P('dp', 'tensor'), may hold values from -0.125 to 0.125
- upproj: bfloat16 [2048, 4096], P('dp', 'tensor'), may hold values from -0.125 to 0.125
- downproj: bfloat16 [2048, 4096], P('dp', 'tensor'), may hold values from -0.1875 to 0.1875
- cotangent: bfloat16 [8192, 2048], P(('dp', 'tensor')), may hold values from -6 to 6
Outputs:
- layer_out: float32 [8192, 2048], P(('dp', 'tensor'))
- grad_residual: float32 [8192, 2048], P(('dp', 'tensor'))
- grad_mixgain: float32 [2048], P(('dp', 'tensor'))
- grad_ffngain: float32 [2048], P(('dp', 'tensor'))
- grad_gateproj: float32 [2048, 3072], P('dp', 'tensor')
- grad_innerproj: float32 [2048, 3072], P('dp', 'tensor')
- grad_stepproj: float32 [2048, 48], P('dp', 'tensor')
- grad_sharedproj: float32 [2048, 512], P(('dp', 'tensor'))
- grad_innerconv: float32 [3072, 4], P('tensor')
- grad_sharedconv: float32 [512, 4], P(('dp', 'tensor'))
- grad_stepbias: float32 [48], P('tensor')
- grad_decaylog: float32 [48], P('tensor')
- grad_skipgain: float32 [48], P('tensor')
- grad_mixerout: float32 [2048, 3072], P('dp', 'tensor')
- grad_queryproj: float32 [2048, 1024], P('dp', 'tensor')
- grad_keyvalue: float32 [2048, 512], P(('dp', 'tensor'))
- grad_attnout: float32 [2048, 1024], P('dp', 'tensor')
- grad_ffngate: float32 [2048, 4096], P('dp', 'tensor')
- grad_upproj: float32 [2048, 4096], P('dp', 'tensor')
- grad_downproj: float32 [2048, 4096], P('dp', 'tensor')
Inputs may be any that keep to these rules, and one draw needn't show every extreme that they name: `segments`: within each sequence the document numbers never fall; a document has 1 to 512 tokens.
All inputs are finite; a program needn't handle non-finite values.
Results may differ from a plain program's by a relative error of at most 0.023.
Values may be sent and summed in bfloat16 or wider, within the bound.
A program may use at most 256 MiB of HBM per device.

v0:
```python
import functools
import math

import jax
import jax.numpy as jnp
import numpy as np
from jax import lax
from jax.experimental import pallas as pl
from jax.experimental.pallas import tpu as pltpu
from jax.sharding import PartitionSpec as P

QUERY_HEADS = 8
KEY_VALUE_HEADS = 2
HEAD_SIZE = 128
SPAN = 256


eps = 1e-05
rope_base = 10000.0


def matrix_product(left, right):
    return jnp.dot(left, right, preferred_element_type=jnp.float32)


def contract_leading_axis(left, right):
    return lax.dot_general(
        left, right, (((0,), (0,)), ((), ())), preferred_element_type=jnp.float32
    )


def contract_last(left, right):
    return lax.dot_general(
        left, right, (((1,), (1,)), ((), ())), preferred_element_type=jnp.float32
    )


def bit_orders(size):
    high = list(range(size.bit_length() - 2, 0, -1))
    return high, high[:2][::-1] + high[2:]


def relative_blocks(size):
    both = []
    for half, order in enumerate(bit_orders(size)):
        chain = [0]
        for bit in order:
            chain = chain + [other ^ (1 << bit) for other in chain]
        both = both + [(other, half) for other in chain]
    return both + [(other ^ 1, half) for other, half in both]


def to_relative(value, axis, size):
    me = lax.axis_index("dp")
    width = value.shape[axis] // (2 * size)
    return jnp.concatenate(
        [
            lax.dynamic_slice_in_dim(value, ((me ^ other) * 2 + half) * width, width, axis)
            for other, half in relative_blocks(size)
        ],
        axis,
    )


def from_relative(value, axis, size):
    me = lax.axis_index("dp")
    width = value.shape[axis] // (2 * size)
    blocks = relative_blocks(size)
    place = jnp.asarray([blocks.index((other, half)) for other in range(size) for half in range(2)], jnp.int32)
    return jnp.concatenate(
        [
            lax.dynamic_slice_in_dim(value, place[(me ^ number) * 2 + half] * width, width, axis)
            for number in range(size)
            for half in range(2)
        ],
        axis,
    )


def after(value, *others):
    return lax.optimization_barrier((value,) + others)[0]


MESH = pl.DeviceIdType.MESH
VMEM_LIMIT = 56 * 1024 * 1024
LINE_CHUNKS = 4
LARGE_LIMIT = 62 * 1024 * 1024


def flip(value, bit):
    unit = 1 << bit
    return value + unit * (1 - 2 * ((value // unit) % 2))


def mixed_with(value, other, bits):
    for bit in range(bits):
        if (other >> bit) & 1:
            value = flip(value, bit)
    return value


def enter(nt, bits):
    me, zed = lax.axis_index("dp"), lax.axis_index("tensor")
    barrier = pltpu.get_barrier_semaphore()
    for other in range(nt):

        @pl.when(zed != other)
        def _(other=other):
            pl.semaphore_signal(barrier, inc=1, device_id=(me, other), device_id_type=MESH)

    for bit in range(bits):
        pl.semaphore_signal(barrier, inc=1, device_id=(flip(me, bit), zed), device_id_type=MESH)
    pl.semaphore_wait(barrier, bits + nt - 1)
    return me, zed


def aligned(start, size):
    return pl.ds(pl.multiple_of(start, 16), size)


def together(*flows):
    flows = [list(flow) for flow in flows]
    order = sorted(
        ((place + 0.5) / len(flow), number, place)
        for number, flow in enumerate(flows)
        for place in range(len(flow))
    )
    for _, number, place in order:
        flows[number][place]()


def gather_steps(nd, me, zed, own, everything, send, recv, local):
    half = own.shape[0] // 2
    blocks = relative_blocks(nd)
    place = {block: number for number, block in enumerate(blocks)}

    def rows(block):
        return everything.at[pl.ds(place[block] * half, half)]

    def source(block):
        return own.at[pl.ds(block[1] * half, half)] if block[0] == 0 else rows(block)

    hops = []
    for part, order in enumerate(bit_orders(nd)):
        chain = [0]
        for bit in order:
            hops = hops + [((other, part), bit) for other in chain]
            chain = chain + [other ^ (1 << bit) for other in chain]
    hops = hops + [(block, 0) for block in blocks[:nd]]

    def copy(number):
        block, bit = hops[number]
        landed = (block[0] ^ (1 << bit), block[1])
        return pltpu.make_async_remote_copy(
            src_ref=source(block),
            dst_ref=rows(landed),
            send_sem=send.at[number],
            recv_sem=recv.at[place[landed]],
            device_id=(flip(me, bit), zed),
            device_id_type=MESH,
        )

    def arrival(block):
        return pltpu.make_async_remote_copy(
            src_ref=rows(block),
            dst_ref=rows(block),
            send_sem=send.at[0],
            recv_sem=recv.at[place[block]],
            device_id=(flip(me, 0), zed),
            device_id_type=MESH,
        )

    def begin():
        for number, (block, bit) in enumerate(hops):
            if block[0] == 0:
                copy(number).start()
        for part in range(2):
            pltpu.make_async_copy(source((0, part)), rows((0, part)), local.at[part]).start()

    def forward(block):
        def step():
            arrival(block).wait_recv()
            for number, (origin, bit) in enumerate(hops):
                if origin == block:
                    copy(number).start()

        return step

    def end():
        for block in blocks[nd:]:
            arrival(block).wait_recv()
        for number in range(len(hops)):
            copy(number).wait_send()
        for part in range(2):
            pltpu.make_async_copy(source((0, part)), rows((0, part)), local.at[part]).wait()

    first, second = blocks[1 : nd // 2], blocks[nd // 2 + 1 : nd]
    middle = [forward(block) for pair in zip(first, second) for block in pair]
    return [begin] + middle + [end]


def gather_hops(nd):
    return 2 * (nd // 2 - 1) + nd


def gather_semaphores(nd):
    return [
        pltpu.SemaphoreType.DMA((gather_hops(nd),)),
        pltpu.SemaphoreType.DMA((2 * nd,)),
        pltpu.SemaphoreType.DMA((2,)),
    ]


def each_rows(rows, body, unit=16):
    def step(number, carry):
        body(aligned(number * unit, unit))
        return carry

    lax.fori_loop(0, rows // unit, step, 0)


def computed_scatter(nd, me, zed, half, compute, stage, held, landed, totals, core_send, core_recv, send, recv):
    chain_length = nd // 2
    block = 256
    pieces = block // half
    per_part = chain_length // pieces
    turns = [part * per_part + spot for spot in range(per_part - 1, -1, -1) for part in range(2)]

    def piece(ref, number):
        return ref.at[pl.ds(number * half, half)]

    def block_of(ref, number):
        return ref.at[pl.ds(number * block, block)]

    rounds, slot = [], 0
    for part, order in enumerate(bit_orders(nd)):
        length, own_rounds = chain_length, []
        for bit in order[::-1]:
            length = length // 2
            own_rounds.append((bit, length, slot))
            slot = slot + length
        rounds.append(own_rounds)

    def core_copy(number):
        return pltpu.make_async_remote_copy(
            src_ref=block_of(stage, number),
            dst_ref=block_of(held, number),
            send_sem=core_send.at[number],
            recv_sem=core_recv.at[number],
            device_id=(flip(me, 0), zed),
            device_id_type=MESH,
        )

    def hop(bit, number, where):
        return pltpu.make_async_remote_copy(
            src_ref=piece(held, number),
            dst_ref=piece(landed, where),
            send_sem=send.at[where],
            recv_sem=recv.at[where],
            device_id=(flip(me, bit), zed),
            device_id_type=MESH,
        )

    def away(number):
        def step():
            compute(nd * half + number * block, None, block_of(stage, number))
            core_copy(number).start()

        return step

    def near(number):
        def step():
            core_copy(number).wait_recv()
            compute(number * block, block_of(held, number), block_of(held, number))
            for inner in range(pieces):
                place = number * pieces + inner
                part, spot = place // chain_length, place % chain_length
                bit, length, first = rounds[part][0]
                if spot >= length:
                    hop(bit, place, first + spot - length).start()

        return step

    def later_sum(part, turn, spot):
        bit, length, first = rounds[part][turn]
        number = part * chain_length + spot

        def step():
            hop(bit, number, first + spot).wait_recv()
            last = turn == len(rounds[part]) - 1

            def body(rows):
                kept, came = piece(held, number)[rows], piece(landed, first + spot)[rows]
                if last:
                    value = kept.astype(jnp.float32) + came.astype(jnp.float32)
                    for target, start, columns in totals:
                        piece(target, part)[rows] = value[:, start : start + columns]
                else:
                    piece(held, number)[rows] = kept + came

            each_rows(half, body)
            if not last:
                next_bit, next_length, next_first = rounds[part][turn + 1]
                if spot >= next_length:
                    hop(next_bit, number, next_first + spot - next_length).start()

        return step

    def end():
        for number in range(len(turns)):
            core_copy(number).wait_send()
        for part in range(2):
            for bit, length, first in rounds[part]:
                for spot in range(length):
                    hop(bit, part * chain_length + length + spot, first + spot).wait_send()

    later = []
    for turn in range(len(rounds[0])):
        length = rounds[0][turn][1]
        later.append([later_sum(part, turn, spot) for spot in range(length - 1, -1, -1) for part in range(2)])
    return [away(number) for number in turns], [near(number) for number in turns], later, end


def computed_scratch(nd, rows, columns):
    slots = nd - 2
    blocks = nd * rows // 2 // 256
    return [
        pltpu.VMEM((nd * rows // 2, columns), jnp.bfloat16),
        pltpu.VMEM((nd * rows // 2, columns), jnp.bfloat16),
        pltpu.VMEM((slots * rows // 2, columns), jnp.bfloat16),
        pltpu.SemaphoreType.DMA((blocks,)),
        pltpu.SemaphoreType.DMA((blocks,)),
        pltpu.SemaphoreType.DMA((slots,)),
        pltpu.SemaphoreType.DMA((slots,)),
    ]


def products_of(left, rights, tile):
    def compute(start, add, target):
        turned_left = jnp.transpose(left[:, start : start + 256])
        at = 0
        for right, columns in rights:
            for first in range(0, columns, tile):
                extent = slice(first, min(first + tile, columns))
                value = jnp.dot(turned_left, right[:, extent], preferred_element_type=jnp.float32)
                here = slice(at + extent.start, at + extent.stop)
                if add is not None:
                    value = value + add[:, here].astype(jnp.float32)
                target[:, here] = value.astype(jnp.bfloat16)
            at = at + columns

    return compute


def line_gather(nt, me, zed, chunks, own, everything, send, recv, chunked=False, reach=None):
    size = own.shape[0] // chunks
    reach = nt - 1 if reach is None else reach

    def own_rows(chunk):
        return own.at[pl.ds(chunk * size, size)]

    def rows(block, chunk):
        start = (chunk * nt + block) * size if chunked else block * (size * chunks) + chunk * size
        return everything.at[aligned(start, size)]

    def copy(source, block, chunk, side):
        return pltpu.make_async_remote_copy(
            src_ref=source,
            dst_ref=rows(block, chunk),
            send_sem=send.at[side, block, chunk],
            recv_sem=recv.at[block, chunk],
            device_id=(me, zed + 1 - 2 * side),
            device_id_type=MESH,
        )

    def keep(chunk):
        return pltpu.make_async_copy(own_rows(chunk), rows(zed, chunk), recv.at[zed, chunk])

    def first(chunk):
        for side, condition in ((0, zed < nt - 1), (1, zed > 0)):

            @pl.when(condition)
            def _(side=side):
                copy(own_rows(chunk), zed, chunk, side).start()

        keep(chunk).start()

    def onward(chunk, distance):
        for side, block in ((0, zed - distance), (1, zed + distance)):
            inside = (block >= 0) if side == 0 else (block < nt)
            open_end = (zed < nt - 1) if side == 0 else (zed > 0)

            @pl.when(inside)
            def _(block=block, side=side):
                copy(rows(block, chunk), block, chunk, side).wait_recv()

            if distance < reach:

                @pl.when(jnp.logical_and(inside, open_end))
                def _(block=block, side=side):
                    copy(rows(block, chunk), block, chunk, side).start()

    def settle(chunk):
        keep(chunk).wait()

    def end(chunk):
        for side, condition in ((0, zed < nt - 1), (1, zed > 0)):

            @pl.when(condition)
            def _(side=side):
                copy(own_rows(chunk), zed, chunk, side).wait_send()

            for distance in range(1, reach):
                block = zed - distance if side == 0 else zed + distance
                inside = (block >= 0) if side == 0 else (block < nt)

                @pl.when(jnp.logical_and(inside, condition))
                def _(block=block, side=side):
                    copy(rows(block, chunk), block, chunk, side).wait_send()

    return first, onward, settle, end


def line_gather_semaphores(nt, chunks):
    return [pltpu.SemaphoreType.DMA((2, nt, chunks)), pltpu.SemaphoreType.DMA((nt, chunks))]


def line_reduce(nt, me, zed, chunks, parts, held, send, recv, chunked=False):
    block_rows = parts.shape[0] // nt
    size = block_rows // chunks
    def rows(block, chunk):
        if chunked:
            return aligned((chunk * nt + block) * size, size)
        return aligned(block * block_rows + chunk * size, size)

    def held_rows(side, block, chunk):
        return aligned((block + 1 - side) * block_rows + chunk * size, size)

    def copy(own, side, block, chunk):
        place = held_rows(side, block, chunk)
        return pltpu.make_async_remote_copy(
            src_ref=parts.at[rows(block, chunk)] if own else held.at[place],
            dst_ref=held.at[place],
            send_sem=send.at[side, block, chunk],
            recv_sem=recv.at[side, block, chunk],
            device_id=(me, zed + 1 - 2 * side),
            device_id_type=MESH,
        )

    def role(side, turn):
        away = nt - 1 - turn
        if side == 0:
            return zed + away, zed + away < nt, zed == 0
        return zed - away, zed - away >= 0, zed == nt - 1

    def pass_on(chunk, turn):
        for side in range(2):
            block, active, source = role(side, turn)

            @pl.when(jnp.logical_and(active, source))
            def _(side=side, block=block):
                copy(True, side, block, chunk).start()

            @pl.when(jnp.logical_and(active, jnp.logical_not(source)))
            def _(side=side, block=block):
                copy(False, side, block, chunk).wait_recv()
                mine, came = parts.at[rows(block, chunk)], held.at[held_rows(side, block, chunk)]

                def body(inner):
                    came[inner] = mine[inner] + came[inner]

                each_rows(size, body)
                copy(False, side, block, chunk).start()

    def own_sum(chunk, total):
        total[...] = parts[rows(zed, chunk)].astype(jnp.float32)
        for side in range(2):

            @pl.when(zed > 0 if side == 0 else zed < nt - 1)
            def _(side=side):
                copy(False, side, zed, chunk).wait_recv()
                total[...] += held[held_rows(side, zed, chunk)].astype(jnp.float32)

    def end(chunk):
        for turn in range(nt - 1):
            for side in range(2):
                block, active, source = role(side, turn)

                @pl.when(active)
                def _(side=side, block=block):
                    copy(False, side, block, chunk).wait_send()

    return pass_on, own_sum, end


def line_reduce_scratch(nt, block_rows, columns, chunks):
    return [
        pltpu.VMEM(((nt + 1) * block_rows, columns), jnp.bfloat16),
        pltpu.VMEM((block_rows // chunks, columns), jnp.float32),
        pltpu.SemaphoreType.DMA((2, nt, chunks)),
        pltpu.SemaphoreType.DMA((2, nt, chunks)),
    ]


HBM = pl.BlockSpec(memory_space=pl.ANY)
ONCHIP = pl.BlockSpec(memory_space=pltpu.VMEM)


def near_first(nt, zed, turn):
    block = 0
    for mine in range(nt):
        order = sorted(range(nt), key=lambda other: (abs(other - mine), other))
        block = block + jnp.where(zed == mine, order[turn], 0)
    return block


def first_gathers(nd, nt, rows, grad, small, main_own, out_own, shared_columns):
    chunks = LINE_CHUNKS
    bits = nd.bit_length() - 1
    blocks = relative_blocks(nd)
    block_rows, width = rows.shape
    lane = width // len(blocks)
    if lane % 128:
        rows, grad = to_relative(rows, 1, nd), to_relative(grad, 1, nd)
    main_columns, small_columns = main_own.shape[1], small.shape[1]
    side_columns = shared_columns + 2 * HEAD_SIZE
    gains_at = shared_columns + 2 * KEY_VALUE_HEADS * HEAD_SIZE
    tile = 256

    def reorder(me, source, target):
        if lane % 128:
            target[...] = source[...]
            return
        for number, (other, part) in enumerate(blocks):
            start = (mixed_with(me, other, bits) * 2 + part) * lane
            target[:, number * lane : (number + 1) * lane] = source[:, pl.ds(pl.multiple_of(start, lane), lane)]

    def kernel(
        rows_in, grad_in, small_ref, main_ref, out_ref,
        rows_ref, grad_ref, gains_ref, normed_all, grad_all, small_line, main_all, side_all, out_all, main_raw, side_raw,
        row_space, normed, main_space, small_space, side_space, main_stage, side_stage, store_sems, *refs,
    ):
        row_sems, small_sems, grad_sems = refs[:2], refs[2:4], refs[4:6]
        main_sems, small_dp, out_sems = refs[6:9], refs[9:12], refs[12:15]
        me, zed = enter(nt, bits)
        small_first, small_onward, small_settle, small_end = line_gather(
            nt, me, zed, 1, small_ref, small_line, *small_sems
        )
        row_first, row_onward, row_settle, row_end = line_gather(
            nt, me, zed, chunks, rows_ref, row_space, *row_sems
        )
        grad_first, grad_onward, grad_settle, grad_end = line_gather(
            nt, me, zed, chunks, grad_ref, grad_all, *grad_sems, chunked=True, reach=1
        )
        main_flow = gather_steps(nd, me, zed, main_ref, main_space, *main_sems)
        small_flow = gather_steps(nd, me, zed, small_line, small_space, *small_dp)
        out_flow = gather_steps(nd, me, zed, out_ref, out_all, *out_sems)
        head = zed * (QUERY_HEADS // nt) // (QUERY_HEADS // KEY_VALUE_HEADS)

        def columns(turn):
            if turn == 0:
                return small_space.at[:, pl.ds(0, shared_columns)], side_space.at[:, pl.ds(0, shared_columns)]
            start = shared_columns + ((turn - 1) * KEY_VALUE_HEADS + head) * HEAD_SIZE
            target = shared_columns + (turn - 1) * HEAD_SIZE
            return (
                small_space.at[:, pl.ds(pl.multiple_of(start, HEAD_SIZE), HEAD_SIZE)],
                side_space.at[:, pl.ds(target, HEAD_SIZE)],
            )

        def keep(number):
            source, target = ((main_space, main_all), (side_space, side_all), (normed, normed_all))[number]
            return pltpu.make_async_copy(source, target, store_sems.at[number])

        def pick(turn):
            return pltpu.make_async_copy(*columns(turn), store_sems.at[3 + turn])

        def store(turn, number):
            block = near_first(nt, zed, turn)
            stage, target = ((main_stage, main_raw), (side_stage, side_raw))[number]
            return pltpu.make_async_copy(
                stage.at[turn % 2],
                target.at[aligned(block * block_rows, block_rows)],
                store_sems.at[6 + 2 * turn + number],
            )

        def project(turn):
            where = aligned(near_first(nt, zed, turn) * block_rows, block_rows)
            value = (rows_ref[...] if turn == 0 else row_space[where]).astype(jnp.float32)
            scale = lax.rsqrt(jnp.mean(value * value, axis=-1, keepdims=True) + eps)
            mine = (value * scale * gains_ref[0:1]).astype(jnp.bfloat16)
            normed[where] = mine
            if turn >= 2:
                store(turn - 2, 0).wait()
                store(turn - 2, 1).wait()
            for space, stage, number in ((main_space, main_stage, 0), (side_space, side_stage, 1)):
                for start in range(0, space.shape[1], tile):
                    extent = slice(start, min(start + tile, space.shape[1]))
                    stage[turn % 2, :, extent] = jnp.dot(
                        mine, space[:, extent], preferred_element_type=jnp.float32
                    )
                store(turn, number).start()

        small_first(0)
        main_flow[0]()
        reorder(me, rows_in, rows_ref)
        for chunk in range(chunks):
            row_first(chunk)
        for distance in range(1, nt):
            small_onward(0, distance)
        small_settle(0)
        small_end(0)
        small_flow[0]()
        out_flow[0]()
        reorder(me, grad_in, grad_ref)
        near = [
            functools.partial(row_onward, chunk, distance) for distance in range(1, nt - 1) for chunk in range(chunks)
        ]
        together(near, main_flow[1:-1] + small_flow[1:-1])
        for chunk in range(chunks):
            grad_first(chunk)
        small_flow[-1]()
        for turn in range(3):
            pick(turn).start()
        for start in range(0, width, 128):
            turned_block = jnp.transpose(
                small_space[start : start + 128, gains_at : gains_at + 128].astype(jnp.float32)
            )
            gains_ref[:, start : start + 128] = turned_block[:8]
        main_flow[-1]()
        keep(0).start()
        for turn in range(3):
            pick(turn).wait()
        keep(1).start()

        def last_rows():
            for chunk in range(chunks):
                row_onward(chunk, nt - 1)

        def grads_from(distance):
            for chunk in range(chunks):
                grad_onward(chunk, distance)

        compute = [functools.partial(project, turn) for turn in range(nt - 1)] + [last_rows]
        together(compute, out_flow[1:-1])
        project(nt - 1)
        keep(2).start()
        grads_from(1)
        out_flow[-1]()
        for chunk in range(chunks):
            row_settle(chunk)
            row_end(chunk)
            grad_settle(chunk)
            grad_end(chunk)
        for turn in range(max(nt - 2, 0), nt):
            store(turn, 0).wait()
            store(turn, 1).wait()
        for number in range(3):
            keep(number).wait()

    def sized(array, times, dtype=None):
        return jax.ShapeDtypeStruct((array.shape[0] * times, array.shape[1]), dtype or array.dtype)

    tokens = block_rows * nt
    return pl.pallas_call(
        kernel,
        out_shape=[
            sized(rows, 1),
            sized(grad, 1),
            jax.ShapeDtypeStruct((8, width), jnp.float32),
            sized(rows, nt),
            sized(grad, nt),
            sized(small, nt),
            sized(main_own, nd),
            jax.ShapeDtypeStruct((width, side_columns), small.dtype),
            sized(out_own, nd),
            jax.ShapeDtypeStruct((tokens, main_columns), jnp.float32),
            jax.ShapeDtypeStruct((tokens, side_columns), jnp.float32),
        ],
        in_specs=[ONCHIP] * 2 + [HBM] * 3,
        out_specs=[ONCHIP] * 3 + [HBM] * 8,
        scratch_shapes=[
            pltpu.VMEM((tokens, width), jnp.bfloat16),
            pltpu.VMEM((tokens, width), jnp.bfloat16),
            pltpu.VMEM((width, main_columns), jnp.bfloat16),
            pltpu.VMEM((width, small_columns), jnp.bfloat16),
            pltpu.VMEM((width, side_columns), jnp.bfloat16),
            pltpu.VMEM((2, block_rows, main_columns), jnp.float32),
            pltpu.VMEM((2, block_rows, side_columns), jnp.float32),
            pltpu.SemaphoreType.DMA((6 + 2 * nt,)),
        ]
        + line_gather_semaphores(nt, chunks)
        + line_gather_semaphores(nt, 1)
        + line_gather_semaphores(nt, chunks)
        + gather_semaphores(nd) * 3,
        compiler_params=pltpu.CompilerParams(
            collective_id=0, has_side_effects=True, vmem_limit_bytes=VMEM_LIMIT
        ),
        name="first_gathers",
    )(rows, grad, small, main_own, out_own)


def second_neighbours(nt, grads):
    zed = lax.axis_index("tensor")
    width = grads.shape[1]
    blocks = grads.reshape(LINE_CHUNKS, nt, -1, width)
    below = lax.dynamic_slice_in_dim(blocks, jnp.maximum(zed - 1, 0), 1, 1).reshape(-1, width)
    above = lax.dynamic_slice_in_dim(blocks, jnp.minimum(zed + 1, nt - 1), 1, 1).reshape(-1, width)
    return (
        lax.ppermute(below, "tensor", [(i, i + 1) for i in range(1, nt - 1)]),
        lax.ppermute(above, "tensor", [(i, i - 1) for i in range(1, nt - 1)]),
    )


def middle_rows(nd, nt, mixed, out_w, resid, gain, grads, grads_below, grads_above, ffn_own):
    chunks = LINE_CHUNKS
    bits = nd.bit_length() - 1
    block_rows, width = resid.shape
    tokens = block_rows * nt
    size = block_rows // chunks
    ffn_columns = ffn_own.shape[1] // 3
    tile = 512

    def kernel(
        mixed_ref, out_ref, resid_ref, gain_ref, grads_ref, below_ref, above_ref, ffn_ref,
        middle_ref, rows_ref, hidden_ref, slopes_ref, grads_all, ffn_all,
        parts, grad_space, ffn_space, own, held, total, send, recv, gather_send, gather_recv,
        ffn_send, ffn_recv, ffn_local, store_sems, far_send, far_recv, far_space, second_sems,
    ):
        me, zed = enter(nt, bits)
        load = pltpu.make_async_copy(grads_ref, grad_space, store_sems.at[0])
        load.start()
        pass_on, own_sum, reduce_end = line_reduce(nt, me, zed, chunks, parts, held, send, recv)
        first, onward, settle, gather_end = line_gather(
            nt, me, zed, chunks, own, rows_ref, gather_send, gather_recv, chunked=True
        )
        flow = gather_steps(nd, me, zed, ffn_ref, ffn_space, ffn_send, ffn_recv, ffn_local)
        keeps = [
            pltpu.make_async_copy(grad_space, grads_all, store_sems.at[1]),
            pltpu.make_async_copy(ffn_space, ffn_all, store_sems.at[2]),
        ]

        def part(turn):
            where = aligned(near_first(nt, zed, nt - 1 - turn) * block_rows, block_rows)
            left = mixed_ref[where]
            for start in range(0, width, tile):
                extent = slice(start, start + tile)
                parts[where, extent] = product(left, out_ref[extent], LAST).astype(jnp.bfloat16)

        def second(action):
            for side, source in ((0, below_ref), (1, above_ref)):

                @pl.when(zed >= 2 if side == 0 else zed < nt - 2)
                def _(side=side, source=source):
                    block = zed - 2 if side == 0 else zed + 2
                    for chunk in range(chunks):
                        place = aligned((chunk * nt + block) * size, size)
                        action(
                            pltpu.make_async_copy(
                                source.at[pl.ds(chunk * size, size)], grad_space.at[place], second_sems.at[side, chunk]
                            )
                        )

        def far(chunk, up):
            block = 0 if up else nt - 1
            return pltpu.make_async_remote_copy(
                src_ref=grad_space.at[pl.ds((chunk * nt + block) * size, size)],
                dst_ref=far_space.at[pl.ds(chunk * size, size)],
                send_sem=far_send.at[chunk],
                recv_sem=far_recv.at[chunk],
                device_id=(me, nt - 1 if up else 0),
                device_id_type=MESH,
            )

        def far_begin():
            for up, sender in ((True, nt - 2), (False, 1)):

                @pl.when(zed == sender)
                def _(up=up):
                    for chunk in range(chunks):
                        far(chunk, up).start()

        def far_end():
            for up, sender in ((True, nt - 2), (False, 1)):

                @pl.when(zed == sender)
                def _(up=up):
                    for chunk in range(chunks):
                        far(chunk, up).wait_send()

                @pl.when(zed == (nt - 1 if up else 0))
                def _(up=up):
                    for chunk in range(chunks):
                        far(chunk, up).wait_recv()
                        start = (chunk * nt + (0 if up else nt - 1)) * size
                        grad_space[pl.ds(start, size)] = far_space[pl.ds(chunk * size, size)]

        def finish(chunk):
            own_sum(chunk, total)
            where = pl.ds(chunk * size, size)
            value = resid_ref[where].astype(jnp.float32) + total[...]
            middle_ref[where] = value
            scale = lax.rsqrt(jnp.mean(value * value, axis=-1, keepdims=True) + eps)
            own[where] = (value * scale * gain_ref[...]).astype(jnp.bfloat16)
            first(chunk)

        def feed(chunk):
            settle(chunk)
            where = pl.ds(chunk * nt * size, nt * size)
            rows, grads = rows_ref[where], grad_space[where]
            for start in range(0, ffn_columns, tile):
                columns = [slice(turn * ffn_columns + start, turn * ffn_columns + start + tile) for turn in range(3)]
                gate = product(rows, ffn_space[:, columns[0]])
                upper = product(rows, ffn_space[:, columns[1]])
                grad = product(grads, ffn_space[:, columns[2]])
                sigma = jax.nn.sigmoid(gate)
                through = gate * sigma
                hidden_ref[where, columns[0]] = (through * upper).astype(jnp.bfloat16)
                slopes_ref[where, columns[0]] = (grad * upper * silu_slope(gate, sigma)).astype(jnp.bfloat16)
                slopes_ref[where, columns[1]] = (grad * through).astype(jnp.bfloat16)

        flow[0]()
        part(0)
        for chunk in range(chunks):
            pass_on(chunk, 0)
        load.wait()
        second(lambda copy: copy.start())
        for turn in range(1, nt):
            part(turn)
        second(lambda copy: copy.wait())
        far_begin()
        ahead = [
            functools.partial(pass_on, 0, turn) for turn in range(1, nt - 1)
        ]
        steps = []

        def add(function, chunk, *rest):
            if 0 <= chunk < chunks:
                steps.append(functools.partial(function, chunk, *rest))

        for chunk in range(1, chunks + 2):
            add(finish, chunk - 1)
            add(onward, chunk - 2, nt - 1)
            for turn in range(1, nt - 1):
                add(pass_on, chunk, turn)
                add(onward, chunk - 1, turn)
            if chunk == 2:
                early = len(steps)
            add(feed, chunk - 2)
        together(ahead + steps[:early], flow[1:] + [far_end])
        for keep in keeps:
            keep.start()
        for step in steps[early:]:
            step()
        for chunk in range(chunks):
            reduce_end(chunk)
            gather_end(chunk)
        for keep in keeps:
            keep.wait()

    return pl.pallas_call(
        kernel,
        out_shape=[
            jax.ShapeDtypeStruct((block_rows, width), jnp.float32),
            jax.ShapeDtypeStruct((tokens, width), jnp.bfloat16),
            jax.ShapeDtypeStruct((tokens, ffn_columns), jnp.bfloat16),
            jax.ShapeDtypeStruct((tokens, 2 * ffn_columns), jnp.bfloat16),
            jax.ShapeDtypeStruct((tokens, width), jnp.bfloat16),
            jax.ShapeDtypeStruct((width, 3 * ffn_columns), jnp.bfloat16),
        ],
        in_specs=[ONCHIP] * 4 + [HBM] * 4,
        out_specs=[ONCHIP] * 4 + [HBM] * 2,
        scratch_shapes=[
            pltpu.VMEM((tokens, width), jnp.bfloat16),
            pltpu.VMEM((tokens, width), jnp.bfloat16),
            pltpu.VMEM((width, 3 * ffn_columns), jnp.bfloat16),
            pltpu.VMEM((block_rows, width), jnp.bfloat16),
        ]
        + line_reduce_scratch(nt, block_rows, width, chunks)
        + line_gather_semaphores(nt, chunks)
        + gather_semaphores(nd)
        + [
            pltpu.SemaphoreType.DMA((3,)),
            pltpu.SemaphoreType.DMA((chunks,)),
            pltpu.SemaphoreType.DMA((chunks,)),
            pltpu.VMEM((block_rows, width), jnp.bfloat16),
            pltpu.SemaphoreType.DMA((2, chunks)),
        ],
        compiler_params=pltpu.CompilerParams(
            collective_id=1, has_side_effects=True, vmem_limit_bytes=LARGE_LIMIT
        ),
        name="middle_rows",
    )(mixed, out_w, resid, gain, grads, grads_below, grads_above, ffn_own)


def absolute_lanes(me, bits, blocks, source, target):
    lane = source.shape[1] // len(blocks)
    for number, (other, part) in enumerate(blocks):
        start = (mixed_with(me, other, bits) * 2 + part) * lane
        target[:, pl.ds(pl.multiple_of(start, lane), lane)] = source[:, number * lane : (number + 1) * lane]


def norm_pull(value, gain, grad):
    scale = lax.rsqrt(jnp.mean(value * value, axis=-1, keepdims=True) + eps)
    scaled = grad * gain
    inner = jnp.mean(scaled * value, axis=-1, keepdims=True)
    return scale * (scaled - value * (inner * scale * scale)), grad * value * scale


def line_steps(nt, chunks, pass_on, finish, onward, settle=None):
    steps = []

    def add(function, chunk, *rest):
        if 0 <= chunk < chunks:
            steps.append(functools.partial(function, chunk, *rest))

    for chunk in range(chunks + 2):
        add(finish, chunk - 1)
        add(onward, chunk - 2, nt - 1)
        for turn in range(1, nt - 1):
            add(pass_on, chunk, turn)
            add(onward, chunk - 1, turn)
    return steps


def middle_back(nd, nt, slopes, hidden, rows, grads, ffn_w, middle, cot, gain):
    chunks = LINE_CHUNKS
    bits = nd.bit_length() - 1
    block_rows, width = middle.shape
    tokens = block_rows * nt
    size = block_rows // chunks
    blocks = relative_blocks(nd)
    lane = width // len(blocks)
    ffn_columns = hidden.shape[1]
    out_rows = width // nd
    tile = 512

    def kernel(
        slopes_in, hidden_in, rows_in, grads_in, ffn_ref, middle_ref, cot_ref, gain_ref,
        grad_ref, gain_out, rows_all, gate_total, up_total, down_total,
        slopes_ref, hidden_ref, rows_ref, grads_ref, weights, load_sems, parts, own, gain_grad,
        line_held, total, send, recv, gather_send, gather_recv, *refs,
    ):
        loads = [
            pltpu.make_async_copy(source, target, load_sems.at[number])
            for number, (source, target) in enumerate(
                (
                    (ffn_ref.at[:, pl.ds(0, 2 * ffn_columns)], weights),
                    (slopes_in, slopes_ref),
                    (rows_in, rows_ref),
                    (hidden_in, hidden_ref),
                    (grads_in, grads_ref),
                )
            )
        ]
        for load in loads:
            load.start()
        me, zed = enter(nt, bits)
        pass_on, own_sum, reduce_end = line_reduce(nt, me, zed, chunks, parts, line_held, send, recv, chunked=True)
        first, onward, settle, gather_end = line_gather(nt, me, zed, chunks, own, rows_all, gather_send, gather_recv)
        half = nd * out_rows // 2
        scatters = [
            computed_scatter(
                nd, me, zed, out_rows // 2, products_of(rows_ref, ((slopes_ref, 2 * ffn_columns),), tile),
                weights.at[pl.ds(0, half)], *refs[:2],
                ((gate_total, 0, ffn_columns), (up_total, ffn_columns, ffn_columns)), *refs[2:6],
            ),
            computed_scatter(
                nd, me, zed, out_rows // 2, products_of(grads_ref, ((hidden_ref, ffn_columns),), tile),
                weights.at[pl.ds(half, half), pl.ds(0, ffn_columns)], *refs[6:8],
                ((down_total, 0, ffn_columns),), *refs[8:12],
            ),
        ]
        gain_grad[...] = jnp.zeros_like(gain_grad)

        def part(chunk):
            where = pl.ds(chunk * nt * size, nt * size)
            left = slopes_ref[where]
            for start in range(0, width, tile):
                extent = slice(start, start + tile)
                parts[where, extent] = product(left, weights[extent], LAST).astype(jnp.bfloat16)

        def finish(chunk):
            own_sum(chunk, total)
            where = pl.ds(chunk * size, size)
            through, gained = norm_pull(middle_ref[where], gain_ref[...], total[...])
            value = cot_ref[where].astype(jnp.float32) + through
            gain_grad[...] += jnp.sum(gained, axis=0, keepdims=True)
            grad_ref[where] = value
            own[where] = value.astype(jnp.bfloat16)
            first(chunk)

        loads[0].wait()
        loads[1].wait()
        for chunk in range(chunks):
            part(chunk)
            pass_on(chunk, 0)
        for load in loads[2:]:
            load.wait()
        over = []
        for number in range(2):
            over = over + [step for pair in zip(scatters[0][number], scatters[1][number]) for step in pair]
        for number in range(len(scatters[0][2])):
            over = over + scatters[0][2][number] + scatters[1][2][number]
        together(line_steps(nt, chunks, pass_on, finish, onward), over)
        for scatter in scatters:
            scatter[3]()
        for chunk in range(chunks):
            reduce_end(chunk)
            settle(chunk)
            gather_end(chunk)
        if lane % 128:
            gain_out[...] = gain_grad[...]
        else:
            absolute_lanes(me, bits, blocks, gain_grad, gain_out)

    results = pl.pallas_call(
        kernel,
        out_shape=[
            jax.ShapeDtypeStruct((block_rows, width), jnp.float32),
            jax.ShapeDtypeStruct((1, width), jnp.float32),
            jax.ShapeDtypeStruct((tokens, width), jnp.bfloat16),
        ]
        + [jax.ShapeDtypeStruct((out_rows, ffn_columns), jnp.float32)] * 3,
        in_specs=[HBM] * 5 + [ONCHIP] * 3,
        out_specs=[ONCHIP, ONCHIP, HBM] + [ONCHIP] * 3,
        scratch_shapes=[
            pltpu.VMEM(slopes.shape, jnp.bfloat16),
            pltpu.VMEM(hidden.shape, jnp.bfloat16),
            pltpu.VMEM(rows.shape, jnp.bfloat16),
            pltpu.VMEM(grads.shape, jnp.bfloat16),
            pltpu.VMEM((width, 2 * ffn_columns), jnp.bfloat16),
            pltpu.SemaphoreType.DMA((5,)),
            pltpu.VMEM((tokens, width), jnp.bfloat16),
            pltpu.VMEM((block_rows, width), jnp.bfloat16),
            pltpu.VMEM((1, width), jnp.float32),
        ]
        + line_reduce_scratch(nt, block_rows, width, chunks)
        + line_gather_semaphores(nt, chunks)
        + computed_scratch(nd, out_rows, 2 * ffn_columns)[1:]
        + computed_scratch(nd, out_rows, ffn_columns)[1:],
        compiler_params=pltpu.CompilerParams(
            collective_id=2, has_side_effects=True, vmem_limit_bytes=LARGE_LIMIT
        ),
        name="middle_back",
    )(slopes, hidden, rows, grads, ffn_w, middle, cot, gain)
    if lane % 128:
        results = (results[0], from_relative(results[1], 1, nd), *results[2:])
    return results


def last_sums(nd, nt, normed, grad_main, grad_side, main, side, resid, before, gain, small, shared_rows, main_widths):
    chunks = LINE_CHUNKS
    bits, line_bits = nd.bit_length() - 1, nt.bit_length() - 1
    block_rows, width = resid.shape
    tokens = block_rows * nt
    size = block_rows // chunks
    blocks = relative_blocks(nd)
    lane = width // len(blocks)
    main_columns, side_columns = main.shape[1], side.shape[1]
    shared_columns = side_columns - 2 * HEAD_SIZE
    side_rows = width // nd
    owned = side_rows // nt
    common_columns = shared_columns + 2 * KEY_VALUE_HEADS * HEAD_SIZE
    count = len(main_widths)
    if lane % 128:
        gain_part = jnp.sum(
            (contract_last(grad_main, main) + contract_last(grad_side, side)) * normed.astype(jnp.float32), axis=0
        )
        own_gain = from_relative(gain_part / gain[0], 0, nd)
        small = jnp.concatenate([own_gain.reshape(-1, 128), small[width // 128 :]])

    def kernel(normed_ref, grad_main_ref, grad_side_ref, main_ref, side_ref, resid_ref, before_ref, gain_ref, small_ref, *refs):
        grad_ref, small_out, common_ref = refs[:3]
        totals, refs = refs[3 : 3 + count], refs[3 + count :]
        parts_ref, side_total, line_held, total, send, recv = refs[:6]
        sums, landed, small_send, small_recv, gain_grad = refs[6:11]
        side_out, side_in, side_send, side_recv = refs[11:15]
        stage, held, hop_landed, core_send, core_recv, hop_send, hop_recv = refs[15:]
        me, zed = enter(nt, bits)
        pass_on, own_sum, reduce_end = line_reduce(nt, me, zed, chunks, parts_ref, line_held, send, recv)
        targets, at = [], 0
        for target, columns in zip(totals, main_widths):
            targets.append((target, at, columns))
            at = at + columns
        targets.append((side_total, main_columns, side_columns))
        away, near, later, scatter_end = computed_scatter(
            nd, me, zed, side_rows // 2,
            products_of(normed_ref, ((grad_main_ref, main_columns), (grad_side_ref, side_columns)), 512),
            stage, held, hop_landed, targets, core_send, core_recv, hop_send, hop_recv,
        )

        def part(turn):
            def step():
                where = aligned(near_first(nt, zed, nt - 1 - turn) * block_rows, block_rows)
                left, right = grad_main_ref[where], grad_side_ref[where]
                for start in range(0, width, 512):
                    extent = slice(start, start + 512)
                    value = product(left, main_ref[extent], LAST) + product(right, side_ref[extent], LAST)
                    parts_ref[where, extent] = value.astype(jnp.bfloat16)

            return step

        def gain_term(number):
            def step():
                if number == 0:
                    gain_grad[...] = jnp.zeros_like(gain_grad)

                def body(inner, carry):
                    where = aligned(number * block_rows + inner * 16, 16)
                    gain_grad[...] += parts_ref[where].astype(jnp.float32) * normed_ref[where].astype(jnp.float32)
                    return carry

                lax.fori_loop(0, block_rows // 16, body, 0)

            return step

        def small_copy(turn):
            if turn < bits:
                device = (flip(me, turn), zed)
            else:
                device = (me, flip(zed, turn - bits))
            extent = slice(None) if turn < bits else pl.ds(0, shared_rows)
            return pltpu.make_async_remote_copy(
                src_ref=sums.at[turn, extent],
                dst_ref=landed.at[turn, extent],
                send_sem=small_send.at[turn],
                recv_sem=small_recv.at[turn],
                device_id=device,
                device_id_type=MESH,
            )

        def small_begin():
            sums[0] = small_ref[...]
            if lane % 128 == 0:
                whole = jnp.sum(gain_grad[...], axis=0, keepdims=True) / gain_ref[...]
                for number, (other, half) in enumerate(blocks):
                    spot = mixed_with(me, other, bits) * 2 + half
                    sums[0, pl.ds(spot, 1), :] = whole[:, number * lane : (number + 1) * lane]
            small_copy(0).start()

        def small_step(turn):
            def step():
                small_copy(turn).wait_recv()
                if turn < bits:
                    sums[turn + 1] = sums[turn] + landed[turn]
                else:
                    sums[turn + 1] = sums[turn]
                    sums[turn + 1, pl.ds(0, shared_rows)] = (
                        sums[turn, pl.ds(0, shared_rows)] + landed[turn, pl.ds(0, shared_rows)]
                    )
                if turn + 1 < bits + line_bits:
                    small_copy(turn + 1).start()

            return step

        def small_end():
            for turn in range(bits + line_bits):
                small_copy(turn).wait_send()
            small_out[...] = sums[bits + line_bits]

        few = [gain_term(number) for number in range(nt if lane % 128 == 0 else 0)]
        few = few + [small_begin] + [small_step(turn) for turn in range(bits + line_bits)]

        def side_copy(source, target):
            return pltpu.make_async_remote_copy(
                src_ref=side_out.at[pl.ds(target * owned, owned)],
                dst_ref=side_in.at[source],
                send_sem=side_send.at[target],
                recv_sem=side_recv.at[source],
                device_id=(me, target),
                device_id_type=MESH,
            )

        def side_begin():
            side_out[...] = side_total[...].astype(jnp.bfloat16)
            for target in range(nt):

                @pl.when(zed != target)
                def _(target=target):
                    side_copy(zed, target).start()

            side_in[zed] = side_out[aligned(zed * owned, owned)]

        def side_end():
            for source in range(nt):

                @pl.when(zed != source)
                def _(source=source):
                    side_copy(source, source).wait_recv()

            common_ref[...] = jnp.zeros_like(common_ref)
            for source in range(nt):
                value = side_in[source].astype(jnp.float32)
                head = source * (QUERY_HEADS // nt) // (QUERY_HEADS // KEY_VALUE_HEADS)
                common_ref[:, :shared_columns] += value[:, :shared_columns]
                for turn in range(2):
                    at = shared_columns + (turn * KEY_VALUE_HEADS + head) * HEAD_SIZE
                    start = shared_columns + turn * HEAD_SIZE
                    common_ref[:, at : at + HEAD_SIZE] += value[:, start : start + HEAD_SIZE]
            for target in range(nt):

                @pl.when(zed != target)
                def _(target=target):
                    side_copy(zed, target).wait_send()

        def finish(chunk):
            own_sum(chunk, total)
            where = pl.ds(chunk * size, size)
            through, _ = norm_pull(resid_ref[where].astype(jnp.float32), gain_ref[...], total[...])
            value = before_ref[where] + through
            if lane % 128:
                grad_ref[where] = value
                return
            for number, (other, half) in enumerate(blocks):
                start = (mixed_with(me, other, bits) * 2 + half) * lane
                grad_ref[where, pl.ds(pl.multiple_of(start, lane), lane)] = value[:, number * lane : (number + 1) * lane]

        def passes(turn):
            return [functools.partial(pass_on, chunk, turn) for chunk in range(chunks)]

        middle = len(away) // 2
        steps = away[:middle] + [part(0)] + passes(0) + away[middle:] + [part(1)] + near[:middle]
        for turn in range(2, nt):
            steps.append(part(turn))
        steps = steps + passes(1) + near[middle:]
        for stage_steps in later[:-1]:
            steps = steps + stage_steps
        for turn in range(2, nt - 1):
            steps = steps + passes(turn)
        steps = steps + few[: -(bits + line_bits)] + later[-1] + [side_begin]
        ends = [functools.partial(finish, chunk) for chunk in range(chunks)]
        rest = few[-(bits + line_bits) :]
        for step in steps:
            step()
        together(ends, rest)
        side_end()
        small_end()
        scatter_end()
        for chunk in range(chunks):
            reduce_end(chunk)

    turns = bits + line_bits
    results = pl.pallas_call(
        kernel,
        out_shape=[
            jax.ShapeDtypeStruct((block_rows, width), jnp.float32),
            jax.ShapeDtypeStruct(small.shape, jnp.float32),
            jax.ShapeDtypeStruct((owned, common_columns), jnp.float32),
        ]
        + [jax.ShapeDtypeStruct((side_rows, columns), jnp.float32) for columns in main_widths],
        in_specs=[ONCHIP] * 9,
        out_specs=[ONCHIP] * (3 + count),
        scratch_shapes=[
            pltpu.VMEM((tokens, width), jnp.bfloat16),
            pltpu.VMEM((side_rows, side_columns), jnp.float32),
        ]
        + line_reduce_scratch(nt, block_rows, width, chunks)
        + [
            pltpu.VMEM((turns + 1, *small.shape), jnp.float32),
            pltpu.VMEM((turns, *small.shape), jnp.float32),
            pltpu.SemaphoreType.DMA((turns,)),
            pltpu.SemaphoreType.DMA((turns,)),
            pltpu.VMEM((16, width), jnp.float32),
            pltpu.VMEM((side_rows, side_columns), jnp.bfloat16),
            pltpu.VMEM((nt, owned, side_columns), jnp.bfloat16),
            pltpu.SemaphoreType.DMA((nt,)),
            pltpu.SemaphoreType.DMA((nt,)),
        ]
        + computed_scratch(nd, side_rows, main_columns + side_columns),
        compiler_params=pltpu.CompilerParams(
            collective_id=3, has_side_effects=True, vmem_limit_bytes=LARGE_LIMIT
        ),
        name="last_sums",
    )(normed, grad_main, grad_side, main, side, resid, before, gain, small)
    if lane % 128:
        results = (from_relative(results[0], 1, nd), *results[1:])
    return results


def silu_slope(value, sig):
    return sig * (1.0 + value * (1.0 - sig))


def split_dot(value, constant, dims, terms):
    total = None
    for _ in range(terms):
        piece = value.astype(jnp.bfloat16)
        value = value - piece.astype(jnp.float32)
        part = lax.dot_general(*((piece, constant) if dims[0] else (constant, piece)), dims[1], preferred_element_type=jnp.float32)
        total = part if total is None else total + part
    return total


PLAIN = (((1,), (0,)), ((), ()))
LAST = (((1,), (1,)), ((), ()))
FIRST = (((0,), (0,)), ((), ()))


def product(left, right, dims=PLAIN):
    return lax.dot_general(left, right, dims, preferred_element_type=jnp.float32)


def turned(value, cosine, sine):
    return value * cosine + pltpu.roll(value, value.shape[-1] // 2, 1) * sine


class Sizes:
    def __init__(self, channels, state_columns, query_columns, heads, length):
        self.channels, self.states = channels, state_columns // 2
        self.query, self.heads, self.length = query_columns, heads, length
        self.span = SPAN
        self.count = length // SPAN
        self.wide = channels + state_columns
        self.head_width = channels // heads
        self.step_at = 2 * channels + query_columns
        self.main = self.step_at + heads + (-(self.step_at + heads)) % 128
        self.step_lanes = self.main - self.step_at
        self.side = state_columns + 2 * HEAD_SIZE
        self.window = min(length, 3 * SPAN)


def spread_heads(size):
    table = np.zeros((size.step_lanes, size.channels), np.float32)
    for head in range(size.heads):
        table[head, head * size.head_width : (head + 1) * size.head_width] = 1.0
    return table.astype(jnp.bfloat16)


def turn_tables(length):
    half = HEAD_SIZE // 2
    angle = np.arange(length, dtype=np.float64)[:, None] * rope_base ** (-np.arange(half) / half)[None]
    cosine, sine = np.cos(angle), np.sin(angle)
    return (
        np.concatenate([cosine, cosine], 1).astype(np.float32),
        np.concatenate([-sine, sine], 1).astype(np.float32),
    )


def token_flags(segments, taps):
    seg = segments[0]
    length = seg.shape[0]
    ends = jnp.broadcast_to(seg.reshape(-1, SPAN)[:, -1:], (length // SPAN, SPAN)).reshape(-1)
    before = jnp.pad(ends, (SPAN, 0), constant_values=-1)[:length]
    lines = [seg == seg]
    lines = lines + [jnp.pad(seg, (lag, 0), constant_values=-1)[:length] == seg for lag in range(1, taps)]
    lines = lines + [before == seg, ends == seg]
    lines = lines + [jnp.pad(seg, (0, lag), constant_values=-1)[lag:] == seg for lag in range(1, taps)]
    lines = lines + [jnp.zeros((length,), bool)] * (16 - len(lines))
    return jnp.stack(lines).astype(jnp.float32).T


def chunk_values(size, taps, main_ref, wide_ref, flags, spread, taps_ref, heads_ref, segc, segr):
    span = size.span
    pre = wide_ref[pl.ds(8, span), :] * taps_ref[0:1, :]
    for lag in range(1, taps):
        pre = pre + wide_ref[pl.ds(8 - lag, span), :] * (flags[:, lag : lag + 1] * taps_ref[lag : lag + 1, :])
    sig = jax.nn.sigmoid(pre)
    act = pre * sig
    inner = act[:, : size.channels]
    bmat = act[:, size.channels : size.channels + size.states].astype(jnp.bfloat16)
    cmat = act[:, size.channels + size.states :].astype(jnp.bfloat16)
    step_in = main_ref[:, size.step_at :] + heads_ref[0:1, :]
    step = jnp.maximum(step_in, 0.0) + jnp.log1p(jnp.exp(-jnp.abs(step_in)))
    logdec = -step * heads_ref[1:2, :]
    rows = lax.broadcasted_iota(jnp.int32, (span, span), 0)
    columns = lax.broadcasted_iota(jnp.int32, (span, span), 1)
    later = jnp.where(rows >= columns, 1.0, 0.0).astype(jnp.bfloat16)
    cumul = split_dot(logdec, later, (False, PLAIN), 3)
    inside = jnp.logical_and(rows >= columns, segc == segr)
    ending = cumul[span - 1 : span, :]
    reach = jnp.exp(cumul) * flags[:, 4:5]
    tail = jnp.exp(ending - cumul) * flags[:, 5:6]
    step_wide = split_dot(step, spread, (True, PLAIN), 2)
    scaled = inner * step_wide
    return dict(
        pre=pre, sig=sig, inner=inner, bmat=bmat, cmat=cmat, step_in=step_in, step=step, logdec=logdec, later=later,
        cumul=cumul, turned=jnp.transpose(cumul), inside=inside, step_wide=step_wide, scaled=scaled,
        scaled_b=scaled.astype(jnp.bfloat16), meeting=product(cmat, bmat, LAST),
        reach_wide=split_dot(reach, spread, (True, PLAIN), 2), tail_wide=split_dot(tail, spread, (True, PLAIN), 2),
        skip_wide=split_dot(jnp.broadcast_to(heads_ref[2:3, :], (8, size.step_lanes)), spread, (True, PLAIN), 2)[0:1],
    )


def decay_of(values, head):
    spread = values["cumul"][:, head : head + 1] - values["turned"][head : head + 1, :]
    return jnp.exp(jnp.where(values["inside"], spread, -1e30))


def softmax_of(size, query, keys, chunk, start, segc, seg_all):
    scores = product(query, keys, LAST) * (1.0 / math.sqrt(HEAD_SIZE))
    rows = lax.broadcasted_iota(jnp.int32, scores.shape, 0) + chunk * size.span
    columns = lax.broadcasted_iota(jnp.int32, scores.shape, 1) + start
    allowed = jnp.logical_and(rows >= columns, segc == seg_all)
    masked = jnp.where(allowed, scores, -1e30)
    expo = jnp.exp(masked - jnp.max(masked, axis=-1, keepdims=True))
    return expo / jnp.sum(expo, axis=-1, keepdims=True)


def mixers_forward(size, taps, main_raw, side_raw, segments, flags, tap_rows, head_rows):
    span = size.span
    per_head = size.head_width

    def kernel(
        main_ref, side_ref, segc_ref, segr_ref, flags_ref, taps_ref, heads_ref, cos_ref, sin_ref, spread_ref,
        mixed_ref, y_ref, state_ref, keys_ref, values_ref, wide, state,
    ):
        chunk = pl.program_id(0)

        @pl.when(chunk == 0)
        def _():
            wide[0:8, :] = jnp.zeros((8, size.wide), jnp.float32)
            state[...] = jnp.zeros_like(state)
            keys_ref[...] = jnp.zeros_like(keys_ref)
            values_ref[...] = jnp.zeros_like(values_ref)

        wide[pl.ds(8, span), : size.channels] = main_ref[:, size.channels : 2 * size.channels]
        wide[pl.ds(8, span), size.channels :] = side_ref[:, : 2 * size.states]
        flags, spread, segc = flags_ref[...], spread_ref[...], segc_ref[...]
        segr = segr_ref[:, pl.ds(pl.multiple_of(chunk * span, span), span)]
        val = chunk_values(size, taps, main_ref, wide, flags, spread, taps_ref, heads_ref, segc, segr)
        wide[0:8, :] = wide[pl.ds(span, 8), :]
        held = state[...]
        held_b = held.astype(jnp.bfloat16)
        state_ref[...] = held
        across = val["reach_wide"] * product(val["cmat"], held_b)
        lane = lax.broadcasted_iota(jnp.int32, (span, 2 * per_head), 1)
        for pair in range(size.heads // 2):
            where = slice(pair * 2 * per_head, (pair + 1) * 2 * per_head)
            both = []
            for head in (2 * pair, 2 * pair + 1):
                weights = (val["meeting"] * decay_of(val, head)).astype(jnp.bfloat16)
                both.append(product(weights, val["scaled_b"][:, where]))
            result = jnp.where(lane < per_head, both[0], both[1])
            result = result + across[:, where] + val["skip_wide"][:, where] * val["inner"][:, where]
            y_ref[:, where] = result
            gate = main_ref[:, where]
            mixed_ref[:, where] = (result * (gate * jax.nn.sigmoid(gate))).astype(jnp.bfloat16)
        keep = jnp.broadcast_to(val["reach_wide"][span - 1 : span, :], (1, size.channels))
        state[...] = keep * held + product(
            val["bmat"], (val["tail_wide"] * val["scaled"]).astype(jnp.bfloat16), FIRST
        )

        cosine, sine = cos_ref[...], sin_ref[...]
        own = pl.ds(pl.multiple_of(chunk * span, span), span)
        key_at = 2 * size.states
        keys_ref[own, :] = turned(side_ref[:, key_at : key_at + HEAD_SIZE], cosine, sine).astype(jnp.bfloat16)
        values_ref[own, :] = side_ref[:, key_at + HEAD_SIZE :].astype(jnp.bfloat16)
        start = pl.multiple_of(jnp.maximum(chunk + 1 - size.window // span, 0) * span, span)
        seen = pl.ds(start, size.window)
        for head in range(size.query // HEAD_SIZE):
            at = 2 * size.channels + head * HEAD_SIZE
            query = turned(main_ref[:, at : at + HEAD_SIZE], cosine, sine).astype(jnp.bfloat16)
            probs = softmax_of(size, query, keys_ref[seen, :], chunk, start, segc, segr_ref[:, seen])
            result = product(probs.astype(jnp.bfloat16), values_ref[seen, :])
            at = size.channels + head * HEAD_SIZE
            mixed_ref[:, at : at + HEAD_SIZE] = result.astype(jnp.bfloat16)

    def rows(columns):
        return pl.BlockSpec((span, columns), lambda i: (i, 0))

    def whole(array):
        return pl.BlockSpec(array.shape, lambda i: (0, 0))

    cosine, sine = turn_tables(size.length)
    spread = spread_heads(size)
    tokens = size.length
    return pl.pallas_call(
        kernel,
        grid=(size.count,),
        in_specs=[
            rows(size.main), rows(size.side), rows(1), whole(segments), rows(16), whole(tap_rows), whole(head_rows),
            rows(HEAD_SIZE), rows(HEAD_SIZE), whole(spread),
        ],
        out_specs=[
            rows(size.channels + size.query), rows(size.channels),
            pl.BlockSpec((size.states, size.channels), lambda i: (i, 0)),
            pl.BlockSpec((tokens, HEAD_SIZE), lambda i: (0, 0)), pl.BlockSpec((tokens, HEAD_SIZE), lambda i: (0, 0)),
        ],
        out_shape=[
            jax.ShapeDtypeStruct((tokens, size.channels + size.query), jnp.bfloat16),
            jax.ShapeDtypeStruct((tokens, size.channels), jnp.float32),
            jax.ShapeDtypeStruct((size.count * size.states, size.channels), jnp.float32),
            jax.ShapeDtypeStruct((tokens, HEAD_SIZE), jnp.bfloat16),
            jax.ShapeDtypeStruct((tokens, HEAD_SIZE), jnp.bfloat16),
        ],
        scratch_shapes=[
            pltpu.VMEM((span + 8, size.wide), jnp.float32),
            pltpu.VMEM((size.states, size.channels), jnp.float32),
        ],
        compiler_params=pltpu.CompilerParams(
            dimension_semantics=("arbitrary",), vmem_limit_bytes=VMEM_LIMIT
        ),
        cost_estimate=pl.CostEstimate(flops=20 * 10**9, bytes_accessed=25 * 10**6, transcendentals=5 * 10**6),
        name="mixers_forward",
    )(main_raw, side_raw, segments.reshape(tokens, 1), segments, flags, tap_rows, head_rows,
      jnp.asarray(cosine), jnp.asarray(sine), jnp.asarray(spread))


def mixers_backward(
    nd, nt, size, taps, grad_mixed, main_raw, side_raw, segments, flags, tap_rows, head_rows, y_value, states, keys, values,
    grad_rows, mixed,
):
    bits = nd.bit_length() - 1
    out_rows, out_columns = grad_rows.shape[1] // nd, mixed.shape[1]
    span = size.span
    per_head = size.head_width
    count = size.count

    def kernel(
        grad_ref, main_ref, side_ref, before_ref, side_before_ref, segc_ref, segr_ref, flags_ref, taps_ref, heads_ref,
        cos_ref, sin_ref, spread_ref, y_ref, state_ref, keys_ref, values_ref, rows_ref, mixed_ref,
        grad_main, grad_side, tap_sums, head_sums, mixer_total, attn_total,
        wide, back, grad_state, grad_keys, grad_values,
        stage, held, landed, core_send, core_recv, hop_send, hop_recv,
    ):
        turn = pl.program_id(0)
        chunk = count - 1 - turn
        me, zed = lax.axis_index("dp"), lax.axis_index("tensor")
        away, near, later, scatter_end = computed_scatter(
            nd, me, zed, out_rows // 2, products_of(rows_ref, ((mixed_ref, out_columns),), 512), stage, held, landed,
            ((mixer_total, 0, size.channels), (attn_total, size.channels, size.query)),
            core_send, core_recv, hop_send, hop_recv,
        )
        stages = [away, near, *later[: count - 3], [step for stage_steps in later[count - 3 :] for step in stage_steps]]
        for number, stage_steps in enumerate(stages):

            @pl.when(turn == number)
            def _(number=number, stage_steps=stage_steps):
                if number == 0:
                    enter(nt, bits)
                for step in stage_steps:
                    step()
                if number == len(stages) - 1:
                    scatter_end()

        @pl.when(turn == 0)
        def _():
            back[pl.ds(span, 8), :] = jnp.zeros((8, size.wide), jnp.float32)
            grad_state[...] = jnp.zeros_like(grad_state)
            grad_keys[...] = jnp.zeros_like(grad_keys)
            grad_values[...] = jnp.zeros_like(grad_values)
            tap_sums[...] = jnp.zeros_like(tap_sums)
            head_sums[...] = jnp.zeros_like(head_sums)

        wide[0:8, : size.channels] = before_ref[...]
        wide[0:8, size.channels :] = side_before_ref[...]
        wide[pl.ds(8, span), : size.channels] = main_ref[:, size.channels : 2 * size.channels]
        wide[pl.ds(8, span), size.channels :] = side_ref[:, : 2 * size.states]
        flags, spread, segc = flags_ref[...], spread_ref[...], segc_ref[...]
        segr = segr_ref[:, pl.ds(pl.multiple_of(chunk * span, span), span)]
        val = chunk_values(size, taps, main_ref, wide, flags, spread, taps_ref, heads_ref, segc, segr)
        inner, scaled = val["inner"], val["scaled"]

        gate = main_ref[:, : size.channels]
        gate_sig = jax.nn.sigmoid(gate)
        grad = grad_ref[:, : size.channels]
        grad_main[:, : size.channels] = (grad * y_ref[...] * silu_slope(gate, gate_sig)).astype(jnp.bfloat16)
        grad_y = grad * (gate * gate_sig)
        grad_y_b = grad_y.astype(jnp.bfloat16)
        tap_sums[4:5, : size.channels] += jnp.sum(grad_y * inner, axis=0, keepdims=True)

        lane = lax.broadcasted_iota(jnp.int32, (span, 2 * per_head), 1)
        head_lane = lax.broadcasted_iota(jnp.int32, (span, size.step_lanes), 1)
        head_row = lax.broadcasted_iota(jnp.int32, (size.step_lanes, span), 0)
        grad_meeting = jnp.zeros((span, span), jnp.float32)
        by_row = jnp.zeros((span, size.step_lanes), jnp.float32)
        by_column = jnp.zeros((size.step_lanes, span), jnp.float32)
        pieces = []
        for pair in range(size.heads // 2):
            where = slice(pair * 2 * per_head, (pair + 1) * 2 * per_head)
            both = []
            for side in range(2):
                head = 2 * pair + side
                decay = decay_of(val, head)
                weights = val["meeting"] * decay
                mine = (lane < per_head) if side == 0 else (lane >= per_head)
                grad_own = jnp.where(mine, grad_y_b[:, where], jnp.zeros((), jnp.bfloat16))
                grad_weights = product(grad_own, val["scaled_b"][:, where], LAST)
                both.append(product(weights.astype(jnp.bfloat16), grad_y_b[:, where], FIRST))
                grad_meeting = grad_meeting + grad_weights * decay
                moved = grad_weights * weights
                by_row = jnp.where(head_lane == head, jnp.sum(moved, axis=1, keepdims=True), by_row)
                by_column = jnp.where(head_row == head, jnp.sum(moved, axis=0, keepdims=True), by_column)
            pieces.append(jnp.where(lane < per_head, both[0], both[1]))
        grad_scaled = jnp.concatenate(pieces, axis=1)
        grad_cumul = by_row - jnp.transpose(by_column)

        held = state_ref[...]
        held_b = held.astype(jnp.bfloat16)
        grad_held = grad_state[...]
        grad_held_b = grad_held.astype(jnp.bfloat16)
        grad_meeting_b = grad_meeting.astype(jnp.bfloat16)
        reached = val["reach_wide"] * grad_y
        reached_b = reached.astype(jnp.bfloat16)
        grad_cumul = grad_cumul + split_dot(reached * product(val["cmat"], held_b), spread, (True, LAST), 2)
        grad_c = product(reached_b, held_b, LAST) + product(grad_meeting_b, val["bmat"])
        from_state = val["tail_wide"] * product(val["bmat"], grad_held_b)
        grad_b = product(grad_meeting_b, val["cmat"], FIRST) + product(
            (val["tail_wide"] * scaled).astype(jnp.bfloat16), grad_held_b, LAST
        )
        grad_scaled = grad_scaled + from_state
        ended = split_dot(scaled * from_state, spread, (True, LAST), 2)
        keep = val["reach_wide"][span - 1 : span, :]
        kept = jnp.sum(grad_held * held, axis=0, keepdims=True) * keep
        kept = split_dot(jnp.broadcast_to(kept, (8, size.channels)), spread, (True, LAST), 2)[0:1]
        at_end = jnp.sum(ended, axis=0, keepdims=True) + kept
        grad_logdec = split_dot(grad_cumul - ended, val["later"], (False, FIRST), 3) + at_end
        grad_state[...] = keep * grad_held + product(val["cmat"], reached_b, FIRST)

        grad_inner = grad_scaled * val["step_wide"] + grad_y * val["skip_wide"]
        grad_step = split_dot(grad_scaled * inner, spread, (True, LAST), 2) - grad_logdec * heads_ref[1:2, :]
        grad_step_raw = grad_step * jax.nn.sigmoid(val["step_in"])
        head_sums[0:1, :] += jnp.sum(grad_step_raw, axis=0, keepdims=True)
        head_sums[1:2, :] += jnp.sum(grad_logdec * val["logdec"], axis=0, keepdims=True)
        grad_main[:, size.step_at :] = grad_step_raw.astype(jnp.bfloat16)

        slope = silu_slope(val["pre"], val["sig"])
        grad_pre = jnp.concatenate([grad_inner, grad_b, grad_c], axis=1) * slope
        back[pl.ds(0, span), :] = grad_pre
        raw = grad_pre * taps_ref[0:1, :]
        tap_sums[0:1, :] += jnp.sum(grad_pre * wide[pl.ds(8, span), :], axis=0, keepdims=True)
        for lag in range(1, taps):
            tap_sums[lag : lag + 1, :] += jnp.sum(
                grad_pre * (wide[pl.ds(8 - lag, span), :] * flags[:, lag : lag + 1]), axis=0, keepdims=True
            )
            raw = raw + back[pl.ds(lag, span), :] * (flags[:, 5 + lag : 6 + lag] * taps_ref[lag : lag + 1, :])
        back[pl.ds(span, 8), :] = back[0:8, :]
        grad_main[:, size.channels : 2 * size.channels] = raw[:, : size.channels].astype(jnp.bfloat16)
        grad_side[:, : 2 * size.states] = raw[:, size.channels :].astype(jnp.bfloat16)

        cosine, sine = cos_ref[...], sin_ref[...]
        start = pl.multiple_of(jnp.maximum(chunk + 1 - size.window // span, 0) * span, span)
        seen = pl.ds(start, size.window)
        seen_keys, seen_values = keys_ref[seen, :], values_ref[seen, :]
        scale = 1.0 / math.sqrt(HEAD_SIZE)
        for head in range(size.query // HEAD_SIZE):
            at = 2 * size.channels + head * HEAD_SIZE
            query = turned(main_ref[:, at : at + HEAD_SIZE], cosine, sine).astype(jnp.bfloat16)
            probs = softmax_of(size, query, seen_keys, chunk, start, segc, segr_ref[:, seen])
            out_at = size.channels + head * HEAD_SIZE
            grad_out = grad_ref[:, out_at : out_at + HEAD_SIZE].astype(jnp.bfloat16)
            grad_probs = product(grad_out, seen_values, LAST)
            delta = jnp.sum(grad_probs * probs, axis=-1, keepdims=True)
            grad_scores = (probs * (grad_probs - delta)).astype(jnp.bfloat16)
            grad_query = product(grad_scores, seen_keys) * scale
            grad_main[:, at : at + HEAD_SIZE] = turned(grad_query, cosine, -sine).astype(jnp.bfloat16)
            grad_keys[seen, :] += product(grad_scores, query, FIRST) * scale
            grad_values[seen, :] += product(probs.astype(jnp.bfloat16), grad_out, FIRST)
        own = pl.ds(pl.multiple_of(chunk * span, span), span)
        key_at = 2 * size.states
        grad_side[:, key_at : key_at + HEAD_SIZE] = turned(grad_keys[own, :], cosine, -sine).astype(jnp.bfloat16)
        grad_side[:, key_at + HEAD_SIZE :] = grad_values[own, :].astype(jnp.bfloat16)

    def rows(columns):
        return pl.BlockSpec((span, columns), lambda i: (count - 1 - i, 0))

    def previous(columns, column):
        return pl.BlockSpec((8, columns), lambda i: (jnp.maximum((count - 1 - i) * (span // 8) - 1, 0), column))

    def whole(array):
        return pl.BlockSpec(array.shape, lambda i: (0, 0))

    cosine, sine = turn_tables(size.length)
    spread = spread_heads(size)
    tokens = size.length
    return pl.pallas_call(
        kernel,
        grid=(count,),
        in_specs=[
            rows(size.channels + size.query), rows(size.main), rows(size.side), previous(size.channels, 1),
            previous(2 * size.states, 0), rows(1), whole(segments), rows(16), whole(tap_rows), whole(head_rows),
            rows(HEAD_SIZE), rows(HEAD_SIZE), whole(spread), rows(size.channels),
            pl.BlockSpec((size.states, size.channels), lambda i: (count - 1 - i, 0)), whole(keys), whole(values),
            whole(grad_rows), whole(mixed),
        ],
        out_specs=[
            rows(size.main), rows(size.side), pl.BlockSpec((8, size.wide), lambda i: (0, 0)),
            pl.BlockSpec((8, size.step_lanes), lambda i: (0, 0)),
            pl.BlockSpec((out_rows, size.channels), lambda i: (0, 0)),
            pl.BlockSpec((out_rows, size.query), lambda i: (0, 0)),
        ],
        out_shape=[
            jax.ShapeDtypeStruct((tokens, size.main), jnp.bfloat16),
            jax.ShapeDtypeStruct((tokens, size.side), jnp.bfloat16),
            jax.ShapeDtypeStruct((8, size.wide), jnp.float32),
            jax.ShapeDtypeStruct((8, size.step_lanes), jnp.float32),
            jax.ShapeDtypeStruct((out_rows, size.channels), jnp.float32),
            jax.ShapeDtypeStruct((out_rows, size.query), jnp.float32),
        ],
        scratch_shapes=[
            pltpu.VMEM((span + 8, size.wide), jnp.float32),
            pltpu.VMEM((span + 8, size.wide), jnp.float32),
            pltpu.VMEM((size.states, size.channels), jnp.float32),
            pltpu.VMEM((tokens, HEAD_SIZE), jnp.float32),
            pltpu.VMEM((tokens, HEAD_SIZE), jnp.float32),
        ]
        + computed_scratch(nd, out_rows, out_columns),
        compiler_params=pltpu.CompilerParams(
            dimension_semantics=("arbitrary",), vmem_limit_bytes=VMEM_LIMIT, collective_id=4, has_side_effects=True
        ),
        cost_estimate=pl.CostEstimate(flops=40 * 10**9, bytes_accessed=60 * 10**6, transcendentals=10**7),
        name="mixers_backward",
    )(grad_mixed, main_raw, side_raw, main_raw, side_raw, segments.reshape(tokens, 1), segments, flags, tap_rows,
      head_rows, jnp.asarray(cosine), jnp.asarray(sine), jnp.asarray(spread), y_value, states, keys, values, grad_rows, mixed)


def per_device(
    nd,
    nt,
    residual,
    segments,
    mixgain,
    ffngain,
    gateproj,
    innerproj,
    stepproj,
    sharedproj,
    innerconv,
    sharedconv,
    stepbias,
    decaylog,
    skipgain,
    mixerout,
    queryproj,
    keyvalue,
    attnout,
    ffngate,
    upproj,
    downproj,
    cotangent,
):
    bfloat = jnp.bfloat16
    single = jnp.float32
    width = residual.shape[1]
    zed = lax.axis_index("tensor")
    seq_count, length = segments.shape
    token_count = seq_count * length
    channels = innerproj.shape[1]
    state_columns = sharedproj.shape[1]
    heads = stepproj.shape[1]
    query_columns = queryproj.shape[1]
    ffn_columns = ffngate.shape[1]
    small_rows = sharedproj.shape[0]
    conv_rows = sharedconv.shape[0]
    taps = sharedconv.shape[1]

    gains = jnp.concatenate(
        [
            mixgain[:, None],
            ffngain[:, None],
            jnp.pad(sharedconv, ((0, small_rows - conv_rows), (0, 0))),
            jnp.zeros((small_rows, 128 - 2 - taps), bfloat),
        ],
        axis=1,
    )
    main_used = 2 * channels + query_columns + heads
    main_own = jnp.concatenate(
        [
            gateproj,
            innerproj,
            queryproj,
            stepproj,
            jnp.zeros((gateproj.shape[0], -main_used % 128), bfloat),
        ],
        axis=1,
    )
    resid_own, cot_own, gain_rows, normed, grad_rows, _, main, side, out_w, main_raw, side_raw = first_gathers(
        nd,
        nt,
        residual,
        cotangent,
        jnp.concatenate([sharedproj, keyvalue, gains], axis=1),
        main_own,
        jnp.concatenate([mixerout, attnout], axis=1),
        state_columns,
    )
    gain_one, gain_two = gain_rows[0], gain_rows[1]
    conv_shared = from_relative(gain_rows[2 : 2 + taps], 1, nd)
    conv_shared = conv_shared.reshape(taps, nd * nt, small_rows)[:, :, :conv_rows].reshape(taps, -1)

    size = Sizes(channels, state_columns, query_columns, heads, length)
    flags = token_flags(segments, taps)
    tap_rows = jnp.concatenate([innerconv.astype(single).T, conv_shared], axis=1)
    tap_rows = jnp.pad(tap_rows, ((0, 8 - taps), (0, 0)))
    head_rows = jnp.stack([stepbias.astype(single), jnp.exp(decaylog.astype(single)), skipgain.astype(single)])
    head_rows = jnp.pad(head_rows, ((0, 5), (0, size.step_lanes - heads)))
    mixed_in, y_value, states, keys, values = mixers_forward(
        size, taps, main_raw, side_raw, segments, flags, tap_rows, head_rows
    )
    middle, rows_two, hidden, grad_gate_up, grad_rows, ffn_w = middle_rows(
        nd,
        nt,
        mixed_in,
        out_w,
        resid_own,
        gain_two[None],
        grad_rows,
        *second_neighbours(nt, grad_rows),
        jnp.concatenate([ffngate, upproj, downproj], axis=1),
    )
    down_w = ffn_w[:, 2 * ffn_columns :]
    grad_middle, grad_gain_two, grad_mix_rows, gate_g, up_g, down_g = middle_back(
        nd, nt, grad_gate_up, hidden, rows_two, grad_rows, ffn_w, middle, cot_own, gain_two[None]
    )
    ffn_part = contract_last(hidden, down_w).astype(bfloat)
    ffn_part = ffn_part.reshape(-1, nt, middle.shape[0] // LINE_CHUNKS, width).swapaxes(0, 1).reshape(token_count, width)
    ffn_part = after(ffn_part, grad_mix_rows)
    ffn_out = lax.psum_scatter(ffn_part, "tensor", scatter_dimension=0, tiled=True)
    layer_out = from_relative(middle + ffn_out.astype(single), 1, nd)
    grad_mixed_in = matrix_product(grad_mix_rows, out_w)
    grad_main, grad_side, tap_sums, head_sums, mixer_g, attn_g = mixers_backward(
        nd, nt, size, taps, grad_mixed_in, main_raw, side_raw, segments, flags, tap_rows, head_rows, y_value, states,
        keys, values, grad_mix_rows, mixed_in,
    )
    small = jnp.concatenate(
        [
            jnp.zeros((width,), single),
            grad_gain_two[0],
            tap_sums[:taps, channels:].reshape(-1),
            tap_sums[:taps, :channels].reshape(-1),
            tap_sums[4, :channels],
            head_sums[:2].reshape(-1),
        ]
    )
    shared_length = 2 * width + taps * state_columns
    small = jnp.pad(small, (0, -small.shape[0] % 1024)).reshape(-1, 128)
    grad_residual, small, common_g, gateproj_g, inner_g, query_g, step_g = last_sums(
        nd,
        nt,
        normed,
        grad_main,
        grad_side,
        main,
        side,
        resid_own,
        grad_middle,
        gain_one[None],
        small,
        shared_length // 128,
        (channels, channels, query_columns, heads),
    )
    small = small.reshape(-1)
    place = lax.axis_index("dp") * nt + zed
    gain_one_g = lax.dynamic_slice_in_dim(small, place * small_rows, small_rows, 0)
    gain_two_g = lax.dynamic_slice_in_dim(small, width + place * small_rows, small_rows, 0)
    conv_g = lax.dynamic_slice_in_dim(
        small[2 * width : shared_length].reshape(taps, -1), place * conv_rows, conv_rows, 1
    ).T
    local = small[shared_length:]
    skip_at = taps * channels
    head_at = skip_at + channels
    return (
        layer_out,
        grad_residual,
        gain_one_g,
        gain_two_g,
        gateproj_g,
        inner_g,
        step_g,
        common_g[:, :state_columns],
        local[:skip_at].reshape(taps, channels).T,
        conv_g,
        local[head_at : head_at + heads],
        local[head_at + size.step_lanes : head_at + size.step_lanes + heads],
        local[skip_at:head_at].reshape(heads, -1).sum(axis=1),
        mixer_g,
        query_g,
        common_g[:, state_columns:],
        attn_g,
        gate_g,
        up_g,
        down_g,
    )


def solution(mesh):
    return jax.shard_map(
        functools.partial(per_device, mesh.shape["dp"], mesh.shape["tensor"]),
        mesh=mesh,
        in_specs=(
            P(("dp", "tensor"), None),
            P("dp", None),
            P(("dp", "tensor")),
            P(("dp", "tensor")),
            P("dp", "tensor"),
            P("dp", "tensor"),
            P("dp", "tensor"),
            P(("dp", "tensor"), None),
            P("tensor", None),
            P(("dp", "tensor"), None),
            P("tensor"),
            P("tensor"),
            P("tensor"),
            P("dp", "tensor"),
            P("dp", "tensor"),
            P(("dp", "tensor"), None),
            P("dp", "tensor"),
            P("dp", "tensor"),
            P("dp", "tensor"),
            P("dp", "tensor"),
            P(("dp", "tensor"), None),
        ),
        out_specs=(
            P(("dp", "tensor"), None),
            P(("dp", "tensor"), None),
            P(("dp", "tensor")),
            P(("dp", "tensor")),
            P("dp", "tensor"),
            P("dp", "tensor"),
            P("dp", "tensor"),
            P(("dp", "tensor"), None),
            P("tensor", None),
            P(("dp", "tensor"), None),
            P("tensor"),
            P("tensor"),
            P("tensor"),
            P("dp", "tensor"),
            P("dp", "tensor"),
            P(("dp", "tensor"), None),
            P("dp", "tensor"),
            P("dp", "tensor"),
            P("dp", "tensor"),
            P("dp", "tensor"),
        ),
        check_vma=False,
    )
```

profile of v0, /device:TPU:0, one launch (start us, length us, event | category | flops | bytes accessed | tf_op | source)
XLA Modules:
  0.0 676.2 jit_solution(1285498889162725229)
XLA Ops:
  7.3 0.8 copy.82
  8.1 0.8 copy.79
  8.9 0.8 copy.80
  9.6 0.8 copy.81
  10.4 1.9 pad_maximum_fusion.1.out_ref
  12.3 2.1 concatenate.25.main_ref
  14.5 0.8 concatenate.24.small_ref
  15.3 127.5 %first_gathers.1 = (bf16[256,2048]{1,0:T(8,128)(2,1)}, bf16[256,2048]{1,0:T(8,128)(2,1)}, f32[8,2048]{1,0:T(8,128)}, bf16[1024,2048]{1,0:T(8,128)(2,1)}, bf16[10...) custom-call(bf16[256,2048]{1,0:T(8,128)(2,1)} %rows_in.1, ...), custom_call_target="tpu_custom_call" | custom-call | tf_op jit(solution)/shard_map/first_gathers/pallas_call | solution.py:664
  142.8 2.7 constant_dynamic-slice_fusion.1
  145.5 1.1 collective-permute-start
  146.7 1.3 collective-permute-start.1
  148.0 0.7 fusion.17
  160.3 0.7 reduce.5
  161.6 1.0 copy.84
  162.6 1.0 copy.85.segc_ref
  164.9 20.1 %mixers_forward.1 = (bf16[1024,1024]{1,0:T(8,128)(2,1)}, f32[1024,768]{1,0:T(8,128)}, f32[1024,768]{1,0:T(8,128)}, bf16[1024,128]{1,0:T(8,128)(2,1)}, bf16[1024,128]{1,0:T(8,128)(2,1)}) custom-call(f32[1024,1920]{1,0:T(8,128)} %get-tuple-element.61.main_ref.before_ref, f32[1024,768]{1,0:T(8,128)} %get-tuple-element.62.side_ref.side_before_ref, ...), custom_call_target="tpu_custom_call" | custom-call | flops 20000000000 | bytes 25000000 | tf_op jit(solution)/shard_map/mixers_forward/pallas_call | solution.py:1467
  185.1 1.2 pad_maximum_fusion.ffn_ref
  186.9 1.0 copy-done.1
  187.9 145.4 %middle_rows.1 = (f32[256,2048]{1,0:T(8,128)}, bf16[1024,2048]{1,0:T(8,128)(2,1)}, bf16[1024,1024]{1,0:T(8,128)(2,1)}, bf16[1024,2048]{1,0:T(8,128)(2,1)}, bf16[...) custom-call(bf16[1024,1024]{1,0:T(8,128)(2,1)} %get-tuple-element.64.mixed_ref, ...), custom_call_target="tpu_custom_call" | custom-call | tf_op jit(solution)/shard_map/middle_rows/pallas_call | solution.py:860
  333.3 7.4 %fusion.2 = bf16[1024,2048]{1,0:T(8,128)(2,1)S(1)} fusion(bf16[1024,1024]{1,0:T(8,128)(2,1)} %get-tuple-element.69.hidden_in, bf16[2048,3072]{1,0:T(8,128)(2,1)} %get-tuple-element.70.ffn_ref), kind=kOutput, calls=%fused_computation.2 | convolution fusion | flops 4297064448 | bytes 10485760 | tf_op jit(solution)/shard_map/dot_general | solution.py:33
  340.7 2.3 copy.88
  342.9 135.6 %middle_back.1 = (f32[256,2048]{1,0:T(8,128)}, f32[1,2048]{1,0:T(1,128)}, bf16[1024,2048]{1,0:T(8,128)(2,1)}, f32[256,1024]{1,0:T(8,128)}, f32[256,1024]{1,0:T(8,128)}, /*index=5*/f32[256,1024]{1,0:T(8,128)}) custom-call(bf16[1024,2048]{1,0:T(8,128)(2,1)} %get-tuple-element.71.slopes_in, bf16[1024,1024]{1,0:T(8,128)(2,1)} %get-tuple-element.69.hidden_in, ...), custom_call_target="tpu_custom_call" | custom-call | tf_op jit(solution)/shard_map/middle_back/pallas_call | solution.py:1016
  478.6 10.0 %fusion.18.grad_ref = f32[1024,1024]{1,0:T(8,128)} fusion(bf16[1024,2048]{1,0:T(8,128)(2,1)} %get-tuple-element.75.rows_ref, bf16[2048,1024]{1,0:T(8,128)(2,1)} %get-tuple-element.65.out_ref), kind=kOutput, calls=%fused_computation.98 | convolution fusion | flops 4294967296 | bytes 12582912 | tf_op jit(solution)/shard_map/dot_general | solution.py:23
  488.7 56.1 %mixers_backward.1 = (bf16[1024,1920]{1,0:T(8,128)(2,1)}, bf16[1024,768]{1,0:T(8,128)(2,1)}, f32[8,1280]{1,0:T(8,128)}, f32[8,128]{1,0:T(8,128)}, f32[256,768]{1,0:T(8,128)}, /*index=5*/f32[256,256]{1,0:T(8,128)}) custom-call(f32[1024,1024]{1,0:T(8,128)} %fusion.18.grad_ref, f32[1024,1920]{1,0:T(8,128)} %get-tuple-element.61.main_ref.before_ref, ...), custom_call_target="tpu_custom_call" | custom-call | flops 40000000000 | bytes 60000000 | tf_op jit(solution)/shard_map/mixers_backward/pallas_call | solution.py:1666
  544.7 0.7 slice.97
  545.5 0.7 slice_bitcast_fusion.1
  546.3 0.8 slice_reduce_fusion
  547.0 0.7 constant_dynamic-update-slice_fusion.17
  548.3 98.3 %last_sums.1 = (f32[256,2048]{1,0:T(8,128)}, f32[80,128]{1,0:T(8,128)}, f32[64,1024]{1,0:T(8,128)}, f32[256,768]{1,0:T(8,128)}, f32[256,768]{1,0:T(8,128)}, /*index=5*/f32[256,256]{1,0:T(8,128)}, f32[256,12]{1,0:T(8,128)}) custom-call(bf16[1024,2048]{1,0:T(8,128)(2,1)} %get-tuple-element.77.normed_ref, bf16[1024,1920]{1,0:T(8,128)(2,1)} %get-tuple-element.82.grad_main_ref, ...), custom_call_target="tpu_custom_call" | custom-call | tf_op jit(solution)/shard_map/last_sums/pallas_call | solution.py:1243
  646.7 0.7 slice.102
  647.4 0.7 slice.101
  648.1 0.7 slice.107
  649.4 1.6 copy.90
  651.7 1.3 fusion.15
  652.9 0.6 fusion.12
  653.6 0.7 slice_bitcast_fusion
  654.8 1.7 fusion.13
  656.5 2.1 convert_add_fusion
  659.2 1.1 copy-done
  660.3 1.3 copy.141
  662.0 0.9 copy.142
  662.9 0.9 copy.143
  663.8 0.9 copy.144
  664.7 0.7 copy.145
  665.4 0.7 copy.146
  666.1 1.0 copy.147
  667.1 1.0 copy.148
  668.0 1.0 copy.149
  (131 shorter events, 6.8 us)
Async XLA Ops:
  7.2 7.3 %copy-start.15 = (bf16[64,512]{1,0:T(8,128)(2,1)S(1)}, bf16[64,512]{1,0:T(8,128)(2,1)}, u32[]{:S(2)}) copy-start(bf16[64,512]{1,0:T(8,128)(2,1)} %param.36) | copy-start | bytes 196612
  7.2 7.3 %copy-start.16 = (bf16[64,512]{1,0:T(8,128)(2,1)S(1)}, bf16[64,512]{1,0:T(8,128)(2,1)}, u32[]{:S(2)}) copy-start(bf16[64,512]{1,0:T(8,128)(2,1)} %param.44) | copy-start | bytes 196612
  7.2 649.3 %reduce-scatter.2.cloned.1.call-start = ((), (), s32[]{:S(2)}) async-start(), calls=%async_computation.1 | async-start | bytes 5242880 | tf_op jit(solution)/shard_map/reduce_scatter | solution.py:1808
  142.7 5.3 copy-start.13
  142.8 16.4 %copy-start.18 = (f32[8,2048]{1,0:T(8,128)S(1)}, f32[8,2048]{1,0:T(8,128)}, u32[]{:S(2)}) copy-start(f32[8,2048]{1,0:T(8,128)} %get-tuple-element.63) | copy-start | bytes 196612
  142.8 17.0 %copy-start.21 = (bf16[768,4]{0,1:T(4,128)(2,1)S(1)}, bf16[768,4]{0,1:T(4,128)(2,1)}, u32[]{:S(2)}) copy-start(bf16[768,4]{0,1:T(4,128)(2,1)} %param.37) | copy-start | bytes 18436
  142.8 17.5 %copy-start.14 = (s32[1,1024]{1,0:T(1,128)S(1)}, s32[1,1024]{1,0:T(1,128)}, u32[]{:S(2)}) copy-start(s32[1,1024]{1,0:T(1,128)} %segr_ref.3) | copy-start | bytes 12292
  142.8 19.8 %copy-start.24 = (bf16[12]{0:T(256)(128)(2,1)S(1)}, bf16[12]{0:T(256)(128)(2,1)}, u32[]{:S(2)}) copy-start(bf16[12]{0:T(256)(128)(2,1)} %param.40) | copy-start | bytes 76
  145.5 18.7 %copy-start.22 = (bf16[12]{0:T(256)(128)(2,1)S(1)}, bf16[12]{0:T(256)(128)(2,1)}, u32[]{:S(2)}) copy-start(bf16[12]{0:T(256)(128)(2,1)} %param.41) | copy-start | bytes 76
  145.5 18.7 %copy-start.23 = (bf16[12]{0:T(256)(128)(2,1)S(1)}, bf16[12]{0:T(256)(128)(2,1)}, u32[]{:S(2)}) copy-start(bf16[12]{0:T(256)(128)(2,1)} %param.39) | copy-start | bytes 76
  145.5 41.4 %collective-permute-start = (bf16[256,2048]{1,0:T(8,128)(2,1)}, bf16[256,2048]{1,0:T(8,128)(2,1)S(1)}, u32[]{:S(2)}, u32[]{:S(2)}) collective-permute-start(bf16[256,2048]{1,0:T(8,128)(2,1)} %bitcast.27), channel_id=1, source_target_pairs={{1,2},{2,3},{5,6},{6,7},{9,10},{10,11},{13,14},{14,15},{17,18},{18... | collective-permute-start | bytes 3145736 | tf_op jit(solution)/shard_map/ppermute | solution.py:709
  146.7 40.3 %collective-permute-start.1 = (bf16[256,2048]{1,0:T(8,128)(2,1)S(1)}, bf16[256,2048]{1,0:T(8,128)(2,1)}, u32[]{:S(2)}, u32[]{:S(2)}) collective-permute-start(bf16[256,2048]{1,0:T(8,128)(2,1)S(1)} %bitcast.70), channel_id=1, source_target_pairs={{1,0},{2,1},{5,4},{6,5},{9,8},{10,9},{13,12},{14,13},{17,16},{18,1... | collective-permute-start | bytes 3145736 | tf_op jit(solution)/shard_map/ppermute | solution.py:710
  164.9 20.1 %copy-start.8 = (bf16[256,1024]{1,0:T(8,128)(2,1)S(1)}, bf16[256,1024]{1,0:T(8,128)(2,1)}, u32[]{:S(2)}) copy-start(bf16[256,1024]{1,0:T(8,128)(2,1)} %param.48) | copy-start | bytes 1572868
  164.9 20.1 %copy-start.9 = (bf16[256,1024]{1,0:T(8,128)(2,1)S(1)}, bf16[256,1024]{1,0:T(8,128)(2,1)}, u32[]{:S(2)}) copy-start(bf16[256,1024]{1,0:T(8,128)(2,1)} %param.47) | copy-start | bytes 1572868
  164.9 20.1 %copy-start.10 = (bf16[256,1024]{1,0:T(8,128)(2,1)S(1)}, bf16[256,1024]{1,0:T(8,128)(2,1)}, u32[]{:S(2)}) copy-start(bf16[256,1024]{1,0:T(8,128)(2,1)} %param.46) | copy-start | bytes 1572868
  186.9 1.0 copy-start.1
  488.7 57.6 %copy-start.20 = (f32[1,2048]{1,0:T(1,128)S(1)}, f32[1,2048]{1,0:T(1,128)}, u32[]{:S(2)}) copy-start(f32[1,2048]{1,0:T(1,128)} %get-tuple-element.87) | copy-start | bytes 24580
  547.7 0.6 copy-start.17
  658.6 1.7 copy-start
  659.2 2.4 copy-start.19
  660.3 1.7 copy-start.7
  660.3 2.6 copy-start.6
  662.0 1.8 copy-start.5
  662.0 2.7 copy-start.12
  662.9 2.5 copy-start.11
  662.9 3.2 copy-start.4
  663.8 3.3 copy-start.3
  666.1 1.9 copy-start.2
Sparse Core Ops, SparseCore 0:
  478.7 74.0 reduce-scatter.1
where the time goes:
time: 687 us; the launch traced here: 676 us
  Pallas kernels  583 us (85%)
  local copies, waits for them, and re-layouts  39.8 us (6%)
  between operations  25.6 us (4%)
  matrix products  17.4 us (3%)
  other arithmetic  7.92 us (1%)
    pallas_call x1, Pallas kernels, middle_rows(): pl.pallas_call(kernel, out_shape=[jax.ShapeDtypeStruct((block_rows, width...  145 us
    pallas_call x1, Pallas kernels, middle_back(): pl.pallas_call(kernel, out_shape=[jax.ShapeDtypeStruct((block_rows, width...  136 us
    pallas_call x1, Pallas kernels, first_gathers(): pl.pallas_call(kernel, out_shape=[sized(rows, 1), sized(grad, 1), jax.Sha...  127 us
    pallas_call x1, Pallas kernels, last_sums(): pl.pallas_call(kernel, out_shape=[jax.ShapeDtypeStruct((block_rows, width...  98.3 us
    pallas_call x1, Pallas kernels, mixers_backward(): pl.pallas_call(kernel, grid=(count,), in_specs=[rows(size.channels + size...  56.1 us
    pallas_call x1, Pallas kernels, mixers_forward(): pl.pallas_call(kernel, grid=(size.count,), in_specs=[rows(size.main), row...  20.1 us
    unnamed x104, local copies, waits for them, and re-layouts  16.6 us
  transfers between devices with their start and end apart: 3, of which 0 were waited for; matrix products, arithmetic and copies ran while one was open for 5% of the time, Pallas kernels for 26%

commit v1 on v0

--- a/solution.py
+++ b/solution.py
@@ -17,16 +17,6 @@
 
 eps = 1e-05
 rope_base = 10000.0
-
-
-def matrix_product(left, right):
-    return jnp.dot(left, right, preferred_element_type=jnp.float32)
-
-
-def contract_leading_axis(left, right):
-    return lax.dot_general(
-        left, right, (((0,), (0,)), ((), ())), preferred_element_type=jnp.float32
-    )
 
 
 def contract_last(left, right):
@@ -48,6 +38,13 @@
             chain = chain + [other ^ (1 << bit) for other in chain]
         both = both + [(other, half) for other in chain]
     return both + [(other ^ 1, half) for other, half in both]
+
+
+def relative_place(other, half, size):
+    place = half * (size // 2) + (other & 1) * size
+    for digit, bit in enumerate(bit_orders(size)[half]):
+        place = place + (((other >> bit) & 1) << digit)
+    return place
 
 
 def to_relative(value, axis, size):
@@ -65,20 +62,14 @@
 def from_relative(value, axis, size):
     me = lax.axis_index("dp")
     width = value.shape[axis] // (2 * size)
-    blocks = relative_blocks(size)
-    place = jnp.asarray([blocks.index((other, half)) for other in range(size) for half in range(2)], jnp.int32)
     return jnp.concatenate(
         [
-            lax.dynamic_slice_in_dim(value, place[(me ^ number) * 2 + half] * width, width, axis)
+            lax.dynamic_slice_in_dim(value, relative_place(me ^ number, half, size) * width, width, axis)
             for number in range(size)
             for half in range(2)
         ],
         axis,
     )
-
-
-def after(value, *others):
-    return lax.optimization_barrier((value,) + others)[0]
 
 
 MESH = pl.DeviceIdType.MESH
@@ -828,28 +819,17 @@
             part(turn)
         second(lambda copy: copy.wait())
         far_begin()
-        ahead = [
-            functools.partial(pass_on, 0, turn) for turn in range(1, nt - 1)
-        ]
-        steps = []
-
-        def add(function, chunk, *rest):
-            if 0 <= chunk < chunks:
-                steps.append(functools.partial(function, chunk, *rest))
-
-        for chunk in range(1, chunks + 2):
-            add(finish, chunk - 1)
-            add(onward, chunk - 2, nt - 1)
-            for turn in range(1, nt - 1):
-                add(pass_on, chunk, turn)
-                add(onward, chunk - 1, turn)
-            if chunk == 2:
-                early = len(steps)
-            add(feed, chunk - 2)
-        together(ahead + steps[:early], flow[1:] + [far_end])
+        steps = line_steps(nt, chunks, pass_on, finish, onward)
+        drain = nt
+        together(steps[:-drain], flow[1:] + [far_end])
         for keep in keeps:
             keep.start()
-        for step in steps[early:]:
+        feeds = [functools.partial(feed, chunk) for chunk in range(chunks)]
+        for number, step in enumerate(steps[-drain:]):
+            if 0 < number < drain and feeds and number - 1 < chunks - 1:
+                feeds.pop(0)()
+            step()
+        for step in feeds:
             step()
         for chunk in range(chunks):
             reduce_end(chunk)
@@ -936,8 +916,9 @@
 
     def kernel(
         slopes_in, hidden_in, rows_in, grads_in, ffn_ref, middle_ref, cot_ref, gain_ref,
-        grad_ref, gain_out, rows_all, gate_total, up_total, down_total,
-        slopes_ref, hidden_ref, rows_ref, grads_ref, weights, load_sems, parts, own, gain_grad,
+        grad_ref, gain_out, rows_all, out_all, gate_total, up_total, down_total,
+        slopes_ref, hidden_ref, rows_ref, grads_ref, weights, down_weights, load_sems, parts, own, gain_grad,
+        out_stage, out_sems,
         line_held, total, send, recv, gather_send, gather_recv, *refs,
     ):
         loads = [
@@ -949,6 +930,7 @@
                     (rows_in, rows_ref),
                     (hidden_in, hidden_ref),
                     (grads_in, grads_ref),
+                    (ffn_ref.at[:, pl.ds(2 * ffn_columns, ffn_columns)], down_weights),
                 )
             )
         ]
@@ -972,6 +954,24 @@
         ]
         gain_grad[...] = jnp.zeros_like(gain_grad)
 
+        def out_copy(chunk, block):
+            return pltpu.make_async_copy(
+                out_stage.at[pl.ds(block * size, size)],
+                out_all.at[pl.ds(block * block_rows + chunk * size, size)],
+                out_sems.at[chunk, block],
+            )
+
+        def feed_out(chunk):
+            if chunk > 0:
+                for block in range(nt):
+                    out_copy(chunk - 1, block).wait()
+            left = hidden_ref[pl.ds(chunk * nt * size, nt * size)]
+            for start in range(0, width, tile):
+                extent = slice(start, start + tile)
+                out_stage[:, extent] = product(left, down_weights[extent], LAST).astype(jnp.bfloat16)
+            for block in range(nt):
+                out_copy(chunk, block).start()
+
         def part(chunk):
             where = pl.ds(chunk * nt * size, nt * size)
             left = slopes_ref[where]
@@ -1001,9 +1001,13 @@
             over = over + [step for pair in zip(scatters[0][number], scatters[1][number]) for step in pair]
         for number in range(len(scatters[0][2])):
             over = over + scatters[0][2][number] + scatters[1][2][number]
+            if number == 0:
+                over = over + [functools.partial(feed_out, chunk) for chunk in range(chunks)]
         together(line_steps(nt, chunks, pass_on, finish, onward), over)
         for scatter in scatters:
             scatter[3]()
+        for block in range(nt):
+            out_copy(chunks - 1, block).wait()
         for chunk in range(chunks):
             reduce_end(chunk)
             settle(chunk)
@@ -1019,20 +1023,24 @@
             jax.ShapeDtypeStruct((block_rows, width), jnp.float32),
             jax.ShapeDtypeStruct((1, width), jnp.float32),
             jax.ShapeDtypeStruct((tokens, width), jnp.bfloat16),
+            jax.ShapeDtypeStruct((tokens, width), jnp.bfloat16),
         ]
         + [jax.ShapeDtypeStruct((out_rows, ffn_columns), jnp.float32)] * 3,
         in_specs=[HBM] * 5 + [ONCHIP] * 3,
-        out_specs=[ONCHIP, ONCHIP, HBM] + [ONCHIP] * 3,
+        out_specs=[ONCHIP, ONCHIP, HBM, HBM] + [ONCHIP] * 3,
         scratch_shapes=[
             pltpu.VMEM(slopes.shape, jnp.bfloat16),
             pltpu.VMEM(hidden.shape, jnp.bfloat16),
             pltpu.VMEM(rows.shape, jnp.bfloat16),
             pltpu.VMEM(grads.shape, jnp.bfloat16),
             pltpu.VMEM((width, 2 * ffn_columns), jnp.bfloat16),
-            pltpu.SemaphoreType.DMA((5,)),
+            pltpu.VMEM((width, ffn_columns), jnp.bfloat16),
+            pltpu.SemaphoreType.DMA((6,)),
             pltpu.VMEM((tokens, width), jnp.bfloat16),
             pltpu.VMEM((block_rows, width), jnp.bfloat16),
             pltpu.VMEM((1, width), jnp.float32),
+            pltpu.VMEM((nt * size, width), jnp.bfloat16),
+            pltpu.SemaphoreType.DMA((chunks, nt)),
         ]
         + line_reduce_scratch(nt, block_rows, width, chunks)
         + line_gather_semaphores(nt, chunks)
@@ -1497,7 +1505,7 @@
 
 
 def mixers_backward(
-    nd, nt, size, taps, grad_mixed, main_raw, side_raw, segments, flags, tap_rows, head_rows, y_value, states, keys, values,
+    nd, nt, size, taps, out_w, main_raw, side_raw, segments, flags, tap_rows, head_rows, y_value, states, keys, values,
     grad_rows, mixed,
 ):
     bits = nd.bit_length() - 1
@@ -1507,10 +1515,10 @@
     count = size.count
 
     def kernel(
-        grad_ref, main_ref, side_ref, before_ref, side_before_ref, segc_ref, segr_ref, flags_ref, taps_ref, heads_ref,
+        out_ref, main_ref, side_ref, before_ref, side_before_ref, segc_ref, segr_ref, flags_ref, taps_ref, heads_ref,
         cos_ref, sin_ref, spread_ref, y_ref, state_ref, keys_ref, values_ref, rows_ref, mixed_ref,
         grad_main, grad_side, tap_sums, head_sums, mixer_total, attn_total,
-        wide, back, grad_state, grad_keys, grad_values,
+        wide, back, grad_state, grad_keys, grad_values, grad_ref,
         stage, held, landed, core_send, core_recv, hop_send, hop_recv,
     ):
         turn = pl.program_id(0)
@@ -1542,6 +1550,10 @@
             tap_sums[...] = jnp.zeros_like(tap_sums)
             head_sums[...] = jnp.zeros_like(head_sums)
 
+        own_rows = rows_ref[pl.ds(pl.multiple_of(chunk * span, span), span), :]
+        for start in range(0, out_columns, 512):
+            extent = slice(start, start + 512)
+            grad_ref[:, extent] = product(own_rows, out_ref[:, extent])
         wide[0:8, : size.channels] = before_ref[...]
         wide[0:8, size.channels :] = side_before_ref[...]
         wide[pl.ds(8, span), : size.channels] = main_ref[:, size.channels : 2 * size.channels]
@@ -1667,7 +1679,7 @@
         kernel,
         grid=(count,),
         in_specs=[
-            rows(size.channels + size.query), rows(size.main), rows(size.side), previous(size.channels, 1),
+            whole(out_w), rows(size.main), rows(size.side), previous(size.channels, 1),
             previous(2 * size.states, 0), rows(1), whole(segments), rows(16), whole(tap_rows), whole(head_rows),
             rows(HEAD_SIZE), rows(HEAD_SIZE), whole(spread), rows(size.channels),
             pl.BlockSpec((size.states, size.channels), lambda i: (count - 1 - i, 0)), whole(keys), whole(values),
@@ -1693,6 +1705,7 @@
             pltpu.VMEM((size.states, size.channels), jnp.float32),
             pltpu.VMEM((tokens, HEAD_SIZE), jnp.float32),
             pltpu.VMEM((tokens, HEAD_SIZE), jnp.float32),
+            pltpu.VMEM((span, out_columns), jnp.float32),
         ]
         + computed_scratch(nd, out_rows, out_columns),
         compiler_params=pltpu.CompilerParams(
@@ -1700,7 +1713,7 @@
         ),
         cost_estimate=pl.CostEstimate(flops=40 * 10**9, bytes_accessed=60 * 10**6, transcendentals=10**7),
         name="mixers_backward",
-    )(grad_mixed, main_raw, side_raw, main_raw, side_raw, segments.reshape(tokens, 1), segments, flags, tap_rows,
+    )(out_w, main_raw, side_raw, main_raw, side_raw, segments.reshape(tokens, 1), segments, flags, tap_rows,
       head_rows, jnp.asarray(cosine), jnp.asarray(sine), jnp.asarray(spread), y_value, states, keys, values, grad_rows, mixed)
 
 
@@ -1798,18 +1811,13 @@
         *second_neighbours(nt, grad_rows),
         jnp.concatenate([ffngate, upproj, downproj], axis=1),
     )
-    down_w = ffn_w[:, 2 * ffn_columns :]
-    grad_middle, grad_gain_two, grad_mix_rows, gate_g, up_g, down_g = middle_back(
+    grad_middle, grad_gain_two, grad_mix_rows, ffn_part, gate_g, up_g, down_g = middle_back(
         nd, nt, grad_gate_up, hidden, rows_two, grad_rows, ffn_w, middle, cot_own, gain_two[None]
     )
-    ffn_part = contract_last(hidden, down_w).astype(bfloat)
-    ffn_part = ffn_part.reshape(-1, nt, middle.shape[0] // LINE_CHUNKS, width).swapaxes(0, 1).reshape(token_count, width)
-    ffn_part = after(ffn_part, grad_mix_rows)
     ffn_out = lax.psum_scatter(ffn_part, "tensor", scatter_dimension=0, tiled=True)
     layer_out = from_relative(middle + ffn_out.astype(single), 1, nd)
-    grad_mixed_in = matrix_product(grad_mix_rows, out_w)
     grad_main, grad_side, tap_sums, head_sums, mixer_g, attn_g = mixers_backward(
-        nd, nt, size, taps, grad_mixed_in, main_raw, side_raw, segments, flags, tap_rows, head_rows, y_value, states,
+        nd, nt, size, taps, out_w, main_raw, side_raw, segments, flags, tap_rows, head_rows, y_value, states,
         keys, values, grad_mix_rows, mixed_in,
     )
     small = jnp.concatenate(

time: 687 us -> 659 us (0.959)
  matrix products: 17.4 us -> 0 us
  between operations: 25.6 us -> 15.1 us
    dot_general x2 -> x0, matrix products: 17.4 us -> none  [the longest x1 10 us: matrix_product(): return jnp.dot(left, right, preferred_element_type=jnp.float32)]
    unnamed x104 -> x102, local copies, waits for them, and re-layouts: 16.6 us -> 16.7 us
  transfers between devices with their start and end apart: 3 -> 3, of which waited for: 0 -> 0; matrix products, arithmetic and copies ran while one was open for 5% -> 3% of each run, Pallas kernels for 26% -> 27%
where the time goes in v1:
time: 659 us; the launch traced here: 648 us
  Pallas kernels  586 us (89%)
  local copies, waits for them, and re-layouts  36.8 us (6%)
  between operations  15.1 us (2%)
  other arithmetic  7.92 us (1%)
    pallas_call x1, Pallas kernels, middle_rows(): pl.pallas_call(kernel, out_shape=[jax.ShapeDtypeStruct((block_rows, width...  143 us
    pallas_call x1, Pallas kernels, middle_back(): pl.pallas_call(kernel, out_shape=[jax.ShapeDtypeStruct((block_rows, width...  137 us
    pallas_call x1, Pallas kernels, first_gathers(): pl.pallas_call(kernel, out_shape=[sized(rows, 1), sized(grad, 1), jax.Sha...  127 us
    pallas_call x1, Pallas kernels, last_sums(): pl.pallas_call(kernel, out_shape=[jax.ShapeDtypeStruct((block_rows, width...  97.6 us
    pallas_call x1, Pallas kernels, mixers_backward(): pl.pallas_call(kernel, grid=(count,), in_specs=[whole(out_w), rows(size.m...  60.3 us
    pallas_call x1, Pallas kernels, mixers_forward(): pl.pallas_call(kernel, grid=(size.count,), in_specs=[rows(size.main), row...  20.1 us
    unnamed x102, local copies, waits for them, and re-layouts  16.7 us
  transfers between devices with their start and end apart: 3, of which 0 were waited for; matrix products, arithmetic and copies ran while one was open for 3% of the time, Pallas kernels for 27%

profile of v1, /device:TPU:0, one launch (start us, length us, event | category | flops | bytes accessed | tf_op | source)
XLA Modules:
  0.0 648.1 jit_solution(7323421794038608540)
XLA Ops:
  7.3 0.8 copy.78
  8.1 0.8 copy.75
  8.9 0.8 copy.76
  9.6 0.8 copy.77
  10.4 1.9 pad_maximum_fusion.1.out_ref
  12.3 2.1 concatenate.25.main_ref
  14.5 0.8 concatenate.24.small_ref
  15.3 127.5 %first_gathers.1 = (bf16[256,2048]{1,0:T(8,128)(2,1)}, bf16[256,2048]{1,0:T(8,128)(2,1)}, f32[8,2048]{1,0:T(8,128)}, bf16[1024,2048]{1,0:T(8,128)(2,1)}, bf16[10...) custom-call(bf16[256,2048]{1,0:T(8,128)(2,1)} %rows_in.1, ...), custom_call_target="tpu_custom_call" | custom-call | tf_op jit(solution)/shard_map/first_gathers/pallas_call | solution.py:655
  142.8 2.7 constant_dynamic-slice_fusion.1
  145.5 1.2 collective-permute-start
  146.7 1.3 collective-permute-start.1
  149.2 0.7 reduce.5
  150.5 1.0 copy.80
  151.5 1.0 copy.81.segc_ref
  152.5 0.6 select_maximum_fusion.taps_ref
  153.8 20.1 %mixers_forward.1 = (bf16[1024,1024]{1,0:T(8,128)(2,1)}, f32[1024,768]{1,0:T(8,128)}, f32[1024,768]{1,0:T(8,128)}, bf16[1024,128]{1,0:T(8,128)(2,1)}, bf16[1024,128]{1,0:T(8,128)(2,1)}) custom-call(f32[1024,1920]{1,0:T(8,128)} %get-tuple-element.61.main_ref.before_ref, f32[1024,768]{1,0:T(8,128)} %get-tuple-element.62.side_ref.side_before_ref, ...), custom_call_target="tpu_custom_call" | custom-call | flops 20000000000 | bytes 25000000 | tf_op jit(solution)/shard_map/mixers_forward/pallas_call | solution.py:1475
  173.9 1.2 pad_maximum_fusion.ffn_ref
  175.2 0.6 fusion.9
  175.8 1.0 copy-done.1
  176.8 143.2 %middle_rows.1 = (f32[256,2048]{1,0:T(8,128)}, bf16[1024,2048]{1,0:T(8,128)(2,1)}, bf16[1024,1024]{1,0:T(8,128)(2,1)}, bf16[1024,2048]{1,0:T(8,128)(2,1)}, bf16[...) custom-call(bf16[1024,1024]{1,0:T(8,128)(2,1)} %get-tuple-element.64.mixed_ref, ...), custom_call_target="tpu_custom_call" | custom-call | tf_op jit(solution)/shard_map/middle_rows/pallas_call | solution.py:840
  320.0 137.0 %middle_back.1 = (f32[256,2048]{1,0:T(8,128)}, f32[1,2048]{1,0:T(1,128)}, bf16[1024,2048]{1,0:T(8,128)(2,1)}, bf16[1024,2048]{1,0:T(8,128)(2,1)}, f32[256,1024]{...) custom-call(bf16[1024,2048]{1,0:T(8,128)(2,1)} %get-tuple-element.69.slopes_in, ...), custom_call_target="tpu_custom_call" | custom-call | tf_op jit(solution)/shard_map/middle_back/pallas_call | solution.py:1020
  457.1 60.3 %mixers_backward.1 = (bf16[1024,1920]{1,0:T(8,128)(2,1)}, bf16[1024,768]{1,0:T(8,128)(2,1)}, f32[8,1280]{1,0:T(8,128)}, f32[8,128]{1,0:T(8,128)}, f32[256,768]{1,0:T(8,128)}, /*index=5*/f32[256,256]{1,0:T(8,128)}) custom-call(bf16[2048,1024]{1,0:T(8,128)(2,1)} %get-tuple-element.65.out_ref, f32[1024,1920]{1,0:T(8,128)} %get-tuple-element.61.main_ref.before_ref, ...), custom_call_target="tpu_custom_call" | custom-call | flops 40000000000 | bytes 60000000 | tf_op jit(solution)/shard_map/mixers_backward/pallas_call | solution.py:1678
  517.3 0.7 slice.93
  518.1 0.7 slice_bitcast_fusion.1
  518.8 0.8 slice_reduce_fusion
  519.6 0.7 constant_dynamic-update-slice_fusion.17
  520.3 0.6 copy-done.16
  520.9 97.6 %last_sums.1 = (f32[256,2048]{1,0:T(8,128)}, f32[80,128]{1,0:T(8,128)}, f32[64,1024]{1,0:T(8,128)}, f32[256,768]{1,0:T(8,128)}, f32[256,768]{1,0:T(8,128)}, /*index=5*/f32[256,256]{1,0:T(8,128)}, f32[256,12]{1,0:T(8,128)}) custom-call(bf16[1024,2048]{1,0:T(8,128)(2,1)} %get-tuple-element.76.normed_ref, bf16[1024,1920]{1,0:T(8,128)(2,1)} %get-tuple-element.82.grad_main_ref, ...), custom_call_target="tpu_custom_call" | custom-call | tf_op jit(solution)/shard_map/last_sums/pallas_call | solution.py:1251
  618.6 0.7 slice.98
  619.3 0.7 slice.97
  620.0 0.7 slice.103
  621.2 1.6 copy.85
  622.9 0.6 reduce_sum.9
  623.5 1.3 fusion.10
  624.8 0.6 fusion.7
  625.5 0.7 slice_bitcast_fusion
  626.7 1.7 fusion.8
  628.4 2.1 convert_add_fusion
  631.1 1.1 copy-done
  632.2 1.3 copy.136
  633.9 0.9 copy.137
  634.7 0.9 copy.138
  635.6 0.9 copy.139
  636.5 0.7 copy.140
  637.2 0.7 copy.141
  637.9 1.0 copy.142
  638.9 1.0 copy.143
  639.9 1.0 copy.144
  (125 shorter events, 4.4 us)
Async XLA Ops:
  7.2 7.3 %copy-start.14 = (bf16[64,512]{1,0:T(8,128)(2,1)S(1)}, bf16[64,512]{1,0:T(8,128)(2,1)}, u32[]{:S(2)}) copy-start(bf16[64,512]{1,0:T(8,128)(2,1)} %param.34) | copy-start | bytes 196612
  7.2 7.3 %copy-start.15 = (bf16[64,512]{1,0:T(8,128)(2,1)S(1)}, bf16[64,512]{1,0:T(8,128)(2,1)}, u32[]{:S(2)}) copy-start(bf16[64,512]{1,0:T(8,128)(2,1)} %param.42) | copy-start | bytes 196612
  7.2 621.2 %reduce-scatter.2.cloned.1.call-start = ((), (), s32[]{:S(2)}) async-start(), calls=%async_computation.1 | async-start | bytes 5242880 | tf_op jit(solution)/shard_map/reduce_scatter | solution.py:1817
  142.7 5.4 copy-start.17
  142.7 5.9 copy-start.20
  142.7 6.4 copy-start.13
  142.8 8.7 %copy-start.23 = (bf16[12]{0:T(256)(128)(2,1)S(1)}, bf16[12]{0:T(256)(128)(2,1)}, u32[]{:S(2)}) copy-start(bf16[12]{0:T(256)(128)(2,1)} %param.38) | copy-start | bytes 76
  145.5 7.7 %copy-start.21 = (bf16[12]{0:T(256)(128)(2,1)S(1)}, bf16[12]{0:T(256)(128)(2,1)}, u32[]{:S(2)}) copy-start(bf16[12]{0:T(256)(128)(2,1)} %param.39) | copy-start | bytes 76
  145.5 7.7 %copy-start.22 = (bf16[12]{0:T(256)(128)(2,1)S(1)}, bf16[12]{0:T(256)(128)(2,1)}, u32[]{:S(2)}) copy-start(bf16[12]{0:T(256)(128)(2,1)} %param.37) | copy-start | bytes 76
  145.5 30.3 %collective-permute-start = (bf16[256,2048]{1,0:T(8,128)(2,1)}, bf16[256,2048]{1,0:T(8,128)(2,1)S(1)}, u32[]{:S(2)}, u32[]{:S(2)}) collective-permute-start(bf16[256,2048]{1,0:T(8,128)(2,1)} %bitcast.11), channel_id=1, source_target_pairs={{1,2},{2,3},{5,6},{6,7},{9,10},{10,11},{13,14},{14,15},{17,18},{18... | collective-permute-start | bytes 3145736 | tf_op jit(solution)/shard_map/ppermute | solution.py:700
  146.7 29.1 %collective-permute-start.1 = (bf16[256,2048]{1,0:T(8,128)(2,1)S(1)}, bf16[256,2048]{1,0:T(8,128)(2,1)}, u32[]{:S(2)}, u32[]{:S(2)}) collective-permute-start(bf16[256,2048]{1,0:T(8,128)(2,1)S(1)} %bitcast.45), channel_id=1, source_target_pairs={{1,0},{2,1},{5,4},{6,5},{9,8},{10,9},{13,12},{14,13},{17,16},{18,1... | collective-permute-start | bytes 3145736 | tf_op jit(solution)/shard_map/ppermute | solution.py:701
  153.8 20.1 %copy-start.8 = (bf16[256,1024]{1,0:T(8,128)(2,1)S(1)}, bf16[256,1024]{1,0:T(8,128)(2,1)}, u32[]{:S(2)}) copy-start(bf16[256,1024]{1,0:T(8,128)(2,1)} %param.46) | copy-start | bytes 1572868
  153.8 20.1 %copy-start.9 = (bf16[256,1024]{1,0:T(8,128)(2,1)S(1)}, bf16[256,1024]{1,0:T(8,128)(2,1)}, u32[]{:S(2)}) copy-start(bf16[256,1024]{1,0:T(8,128)(2,1)} %param.45) | copy-start | bytes 1572868
  153.8 20.2 %copy-start.10 = (bf16[256,1024]{1,0:T(8,128)(2,1)S(1)}, bf16[256,1024]{1,0:T(8,128)(2,1)}, u32[]{:S(2)}) copy-start(bf16[256,1024]{1,0:T(8,128)(2,1)} %param.44) | copy-start | bytes 1572868
  175.8 1.0 copy-start.1
  457.0 61.8 %copy-start.19 = (f32[1,2048]{1,0:T(1,128)S(1)}, f32[1,2048]{1,0:T(1,128)}, u32[]{:S(2)}) copy-start(f32[1,2048]{1,0:T(1,128)} %get-tuple-element.87) | copy-start | bytes 24580
  520.3 0.6 copy-start.16
  630.5 1.7 copy-start
  631.1 2.4 copy-start.18
  632.2 1.7 copy-start.7
  632.2 2.6 copy-start.6
  633.9 1.8 copy-start.5
  633.9 2.7 copy-start.12
  634.7 2.5 copy-start.11
  634.7 3.2 copy-start.4
  635.6 3.3 copy-start.3
  637.9 1.9 copy-start.2
Sparse Core Ops, SparseCore 0:
  457.1 76.5 reduce-scatter.1

commit v2 on v1

--- a/solution.py
+++ b/solution.py
@@ -606,9 +606,9 @@
         near = [
             functools.partial(row_onward, chunk, distance) for distance in range(1, nt - 1) for chunk in range(chunks)
         ]
-        together(near, main_flow[1:-1] + small_flow[1:-1])
         for chunk in range(chunks):
             grad_first(chunk)
+        together(near, main_flow[1:-1] + small_flow[1:-1])
         small_flow[-1]()
         for turn in range(3):
             pick(turn).start()

time: 659 us -> 653 us (level)
    pallas_call x1, Pallas kernels: 127 us -> 117 us  [first_gathers(): pl.pallas_call(kernel, out_shape=[sized(rows, 1), sized(grad, 1), jax.Sha...]
  transfers between devices with their start and end apart: 3 -> 3, of which waited for: 0 -> 0; matrix products, arithmetic and copies ran while one was open for 3% -> 3% of each run, Pallas kernels for 27% -> 28%
where the time goes in v2:
time: 653 us; the launch traced here: 643 us
  Pallas kernels  580 us (89%)
  local copies, waits for them, and re-layouts  36.8 us (6%)
  between operations  15.1 us (2%)
  other arithmetic  7.92 us (1%)
    pallas_call x1, Pallas kernels, middle_rows(): pl.pallas_call(kernel, out_shape=[jax.ShapeDtypeStruct((block_rows, width...  143 us
    pallas_call x1, Pallas kernels, middle_back(): pl.pallas_call(kernel, out_shape=[jax.ShapeDtypeStruct((block_rows, width...  143 us
    pallas_call x1, Pallas kernels, first_gathers(): pl.pallas_call(kernel, out_shape=[sized(rows, 1), sized(grad, 1), jax.Sha...  117 us
    pallas_call x1, Pallas kernels, last_sums(): pl.pallas_call(kernel, out_shape=[jax.ShapeDtypeStruct((block_rows, width...  99.7 us
    pallas_call x1, Pallas kernels, mixers_backward(): pl.pallas_call(kernel, grid=(count,), in_specs=[whole(out_w), rows(size.m...  58.2 us
    pallas_call x1, Pallas kernels, mixers_forward(): pl.pallas_call(kernel, grid=(size.count,), in_specs=[rows(size.main), row...  20.1 us
    unnamed x102, local copies, waits for them, and re-layouts  16.7 us
  transfers between devices with their start and end apart: 3, of which 0 were waited for; matrix products, arithmetic and copies ran while one was open for 3% of the time, Pallas kernels for 28%

profile of v2, /device:TPU:0, one launch (start us, length us, event | category | flops | bytes accessed | tf_op | source)
XLA Modules:
  0.0 642.7 jit_solution(1330837357894561341)
XLA Ops:
  7.3 0.8 copy.78
  8.1 0.8 copy.75
  8.9 0.8 copy.76
  9.6 0.8 copy.77
  10.4 1.9 pad_maximum_fusion.1.out_ref
  12.3 2.1 concatenate.25.main_ref
  14.5 0.8 concatenate.24.small_ref
  15.3 117.2 %first_gathers.1 = (bf16[256,2048]{1,0:T(8,128)(2,1)}, bf16[256,2048]{1,0:T(8,128)(2,1)}, f32[8,2048]{1,0:T(8,128)}, bf16[1024,2048]{1,0:T(8,128)(2,1)}, bf16[10...) custom-call(bf16[256,2048]{1,0:T(8,128)(2,1)} %rows_in.1, ...), custom_call_target="tpu_custom_call" | custom-call | tf_op jit(solution)/shard_map/first_gathers/pallas_call | solution.py:655
  132.5 2.7 constant_dynamic-slice_fusion.1
  135.2 1.2 collective-permute-start
  136.4 1.3 collective-permute-start.1
  138.9 0.7 reduce.5
  140.2 1.0 copy.80
  141.2 1.0 copy.81.segc_ref
  142.3 0.6 select_maximum_fusion.taps_ref
  143.5 20.1 %mixers_forward.1 = (bf16[1024,1024]{1,0:T(8,128)(2,1)}, f32[1024,768]{1,0:T(8,128)}, f32[1024,768]{1,0:T(8,128)}, bf16[1024,128]{1,0:T(8,128)(2,1)}, bf16[1024,128]{1,0:T(8,128)(2,1)}) custom-call(f32[1024,1920]{1,0:T(8,128)} %get-tuple-element.61.main_ref.before_ref, f32[1024,768]{1,0:T(8,128)} %get-tuple-element.62.side_ref.side_before_ref, ...), custom_call_target="tpu_custom_call" | custom-call | flops 20000000000 | bytes 25000000 | tf_op jit(solution)/shard_map/mixers_forward/pallas_call | solution.py:1475
  163.7 1.2 pad_maximum_fusion.ffn_ref
  164.9 0.6 fusion.9
  165.5 1.0 copy-done.1
  166.5 142.6 %middle_rows.1 = (f32[256,2048]{1,0:T(8,128)}, bf16[1024,2048]{1,0:T(8,128)(2,1)}, bf16[1024,1024]{1,0:T(8,128)(2,1)}, bf16[1024,2048]{1,0:T(8,128)(2,1)}, bf16[...) custom-call(bf16[1024,1024]{1,0:T(8,128)(2,1)} %get-tuple-element.64.mixed_ref, ...), custom_call_target="tpu_custom_call" | custom-call | tf_op jit(solution)/shard_map/middle_rows/pallas_call | solution.py:840
  309.1 142.5 %middle_back.1 = (f32[256,2048]{1,0:T(8,128)}, f32[1,2048]{1,0:T(1,128)}, bf16[1024,2048]{1,0:T(8,128)(2,1)}, bf16[1024,2048]{1,0:T(8,128)(2,1)}, f32[256,1024]{...) custom-call(bf16[1024,2048]{1,0:T(8,128)(2,1)} %get-tuple-element.69.slopes_in, ...), custom_call_target="tpu_custom_call" | custom-call | tf_op jit(solution)/shard_map/middle_back/pallas_call | solution.py:1020
  451.7 58.2 %mixers_backward.1 = (bf16[1024,1920]{1,0:T(8,128)(2,1)}, bf16[1024,768]{1,0:T(8,128)(2,1)}, f32[8,1280]{1,0:T(8,128)}, f32[8,128]{1,0:T(8,128)}, f32[256,768]{1,0:T(8,128)}, /*index=5*/f32[256,256]{1,0:T(8,128)}) custom-call(bf16[2048,1024]{1,0:T(8,128)(2,1)} %get-tuple-element.65.out_ref, f32[1024,1920]{1,0:T(8,128)} %get-tuple-element.61.main_ref.before_ref, ...), custom_call_target="tpu_custom_call" | custom-call | flops 40000000000 | bytes 60000000 | tf_op jit(solution)/shard_map/mixers_backward/pallas_call | solution.py:1678
  509.9 0.7 slice.93
  510.6 0.7 slice_bitcast_fusion.1
  511.4 0.8 slice_reduce_fusion
  512.2 0.7 constant_dynamic-update-slice_fusion.17
  512.8 0.6 copy-done.16
  513.5 99.7 %last_sums.1 = (f32[256,2048]{1,0:T(8,128)}, f32[80,128]{1,0:T(8,128)}, f32[64,1024]{1,0:T(8,128)}, f32[256,768]{1,0:T(8,128)}, f32[256,768]{1,0:T(8,128)}, /*index=5*/f32[256,256]{1,0:T(8,128)}, f32[256,12]{1,0:T(8,128)}) custom-call(bf16[1024,2048]{1,0:T(8,128)(2,1)} %get-tuple-element.76.normed_ref, bf16[1024,1920]{1,0:T(8,128)(2,1)} %get-tuple-element.82.grad_main_ref, ...), custom_call_target="tpu_custom_call" | custom-call | tf_op jit(solution)/shard_map/last_sums/pallas_call | solution.py:1251
  613.2 0.7 slice.98
  613.9 0.7 slice.97
  614.6 0.7 slice.103
  615.9 1.6 copy.85
  617.5 0.6 reduce_sum.9
  618.2 1.3 fusion.10
  619.4 0.6 fusion.7
  620.1 0.7 slice_bitcast_fusion
  621.3 1.7 fusion.8
  623.0 2.1 convert_add_fusion
  625.7 1.1 copy-done
  626.8 1.3 copy.136
  628.5 0.9 copy.137
  629.4 0.9 copy.138
  630.3 0.9 copy.139
  631.1 0.7 copy.140
  631.8 0.7 copy.141
  632.5 1.0 copy.142
  633.5 1.0 copy.143
  634.5 1.0 copy.144
  (125 shorter events, 4.4 us)
Async XLA Ops:
  7.2 7.3 %copy-start.14 = (bf16[64,512]{1,0:T(8,128)(2,1)S(1)}, bf16[64,512]{1,0:T(8,128)(2,1)}, u32[]{:S(2)}) copy-start(bf16[64,512]{1,0:T(8,128)(2,1)} %param.34) | copy-start | bytes 196612
  7.2 7.3 %copy-start.15 = (bf16[64,512]{1,0:T(8,128)(2,1)S(1)}, bf16[64,512]{1,0:T(8,128)(2,1)}, u32[]{:S(2)}) copy-start(bf16[64,512]{1,0:T(8,128)(2,1)} %param.42) | copy-start | bytes 196612
  7.2 615.8 %reduce-scatter.2.cloned.1.call-start = ((), (), s32[]{:S(2)}) async-start(), calls=%async_computation.1 | async-start | bytes 5242880 | tf_op jit(solution)/shard_map/reduce_scatter | solution.py:1817
  132.4 5.4 copy-start.17
  132.4 5.9 copy-start.20
  132.5 6.4 %copy-start.13 = (s32[1,1024]{1,0:T(1,128)S(1)}, s32[1,1024]{1,0:T(1,128)}, u32[]{:S(2)}) copy-start(s32[1,1024]{1,0:T(1,128)} %segr_ref.3) | copy-start | bytes 12292
  132.5 8.7 %copy-start.23 = (bf16[12]{0:T(256)(128)(2,1)S(1)}, bf16[12]{0:T(256)(128)(2,1)}, u32[]{:S(2)}) copy-start(bf16[12]{0:T(256)(128)(2,1)} %param.38) | copy-start | bytes 76
  135.2 7.7 %copy-start.21 = (bf16[12]{0:T(256)(128)(2,1)S(1)}, bf16[12]{0:T(256)(128)(2,1)}, u32[]{:S(2)}) copy-start(bf16[12]{0:T(256)(128)(2,1)} %param.39) | copy-start | bytes 76
  135.2 7.7 %copy-start.22 = (bf16[12]{0:T(256)(128)(2,1)S(1)}, bf16[12]{0:T(256)(128)(2,1)}, u32[]{:S(2)}) copy-start(bf16[12]{0:T(256)(128)(2,1)} %param.37) | copy-start | bytes 76
  135.2 30.3 %collective-permute-start = (bf16[256,2048]{1,0:T(8,128)(2,1)}, bf16[256,2048]{1,0:T(8,128)(2,1)S(1)}, u32[]{:S(2)}, u32[]{:S(2)}) collective-permute-start(bf16[256,2048]{1,0:T(8,128)(2,1)} %bitcast.11), channel_id=1, source_target_pairs={{1,2},{2,3},{5,6},{6,7},{9,10},{10,11},{13,14},{14,15},{17,18},{18... | collective-permute-start | bytes 3145736 | tf_op jit(solution)/shard_map/ppermute | solution.py:700
  136.4 29.1 %collective-permute-start.1 = (bf16[256,2048]{1,0:T(8,128)(2,1)S(1)}, bf16[256,2048]{1,0:T(8,128)(2,1)}, u32[]{:S(2)}, u32[]{:S(2)}) collective-permute-start(bf16[256,2048]{1,0:T(8,128)(2,1)S(1)} %bitcast.45), channel_id=1, source_target_pairs={{1,0},{2,1},{5,4},{6,5},{9,8},{10,9},{13,12},{14,13},{17,16},{18,1... | collective-permute-start | bytes 3145736 | tf_op jit(solution)/shard_map/ppermute | solution.py:701
  143.5 20.1 %copy-start.8 = (bf16[256,1024]{1,0:T(8,128)(2,1)S(1)}, bf16[256,1024]{1,0:T(8,128)(2,1)}, u32[]{:S(2)}) copy-start(bf16[256,1024]{1,0:T(8,128)(2,1)} %param.46) | copy-start | bytes 1572868
  143.5 20.1 %copy-start.9 = (bf16[256,1024]{1,0:T(8,128)(2,1)S(1)}, bf16[256,1024]{1,0:T(8,128)(2,1)}, u32[]{:S(2)}) copy-start(bf16[256,1024]{1,0:T(8,128)(2,1)} %param.45) | copy-start | bytes 1572868
  143.5 20.1 %copy-start.10 = (bf16[256,1024]{1,0:T(8,128)(2,1)S(1)}, bf16[256,1024]{1,0:T(8,128)(2,1)}, u32[]{:S(2)}) copy-start(bf16[256,1024]{1,0:T(8,128)(2,1)} %param.44) | copy-start | bytes 1572868
  165.5 1.0 copy-start.1
  451.7 59.7 %copy-start.19 = (f32[1,2048]{1,0:T(1,128)S(1)}, f32[1,2048]{1,0:T(1,128)}, u32[]{:S(2)}) copy-start(f32[1,2048]{1,0:T(1,128)} %get-tuple-element.87) | copy-start | bytes 24580
  512.8 0.6 copy-start.16
  625.1 1.7 copy-start
  625.7 2.4 copy-start.18
  626.8 1.7 copy-start.7
  626.8 2.6 copy-start.6
  628.5 1.8 copy-start.5
  628.5 2.7 copy-start.12
  629.4 2.5 copy-start.11
  629.4 3.2 copy-start.4
  630.3 3.3 copy-start.3
  632.5 1.9 copy-start.2
Sparse Core Ops, SparseCore 0:
  451.8 72.6 reduce-scatter.1
